TPU v7x, 32 devices: a whole 2x2x4 slice. The times are simulated.
32 devices in a mesh: gx: 4 (over x, core), gy: 2 (over y), ha: 4 (over z).
Axes of the slice: x: 2, y: 2, z: 4, core: 2. Of those that a mesh axis runs over, the one named last changes fastest.
Arguments:
- initial_value: float32 [64, 32, 4096], P('gx', 'gy', 'ha'), may hold values from -6 to 6
- corner: int32 [32, 4, 32], P(('gx', 'gy', 'ha')), may hold values from -1 to 244670, as said below
- weights: float32 [32, 16, 4, 32], P(('gx', 'gy', 'ha')), may hold values from 0 to 0.125
Outputs:
- final_value: float32 [64, 32, 4096], P('gx', 'gy', 'ha')
- sample_values: float32 [32, 4, 32], P(('gx', 'gy', 'ha'))
Inputs may be any that keep to these rules, and one draw needn't show every extreme that they name: A live corner is ((a 16 + b) * 16 + k) * 64 + v with a <= 14, b <= 14, k <= 14, v <= 62; -1 marks an empty slot; in each bucket [s, :, o] the live slots come first; in every draw some owner's buckets are full from every source.
All inputs are finite; a program needn't handle non-finite values.
Results may differ from a plain program's by a relative error of at most 0.0003.
Values sent between devices are 32-bit elements; how exact they have to be, the bound alone decides.
A program may use at most 64 MiB of HBM per device.

v0:
```python
import math

import jax
import jax.numpy as jnp
from jax import lax
from jax.sharding import PartitionSpec as P

NV = 64
STEPS = 4


epsilon = 1e-06
turn_rate = 1.0
time_step = 0.15
two_pi = 6.283185307179586


def extended(cells, sides, width, closed):
    for axis, dim in sides:
        count = lax.axis_size(axis)
        ends = count if closed else count - 1
        head = lax.slice_in_dim(cells, 0, width, axis=dim)
        tail = lax.slice_in_dim(cells, cells.shape[dim] - width, cells.shape[dim], axis=dim)
        cells = jnp.concatenate(
            [
                lax.ppermute(tail, axis, [(i, (i + 1) % count) for i in range(ends)]),
                cells,
                lax.ppermute(head, axis, [((i + 1) % count, i) for i in range(ends)]),
            ],
            axis=dim,
        )
    return cells


def window_of(array_in, begin_at, length_of, along, stride):
    return lax.slice_in_dim(
        array_in, begin_at * stride, (begin_at + length_of) * stride, axis=along
    )


def blend(outer_low, inner_low, center, inner_high, outer_high):
    guess_one = outer_low / 3.0 - 7.0 * inner_low / 6.0 + 11.0 * center / 6.0
    guess_two = -inner_low / 6.0 + 5.0 * center / 6.0 + inner_high / 3.0
    guess_three = center / 3.0 + 5.0 * inner_high / 6.0 - outer_high / 6.0
    rough_one = (
        13.0 / 12.0 * (outer_low - 2.0 * inner_low + center) ** 2
        + 0.25 * (outer_low - 4.0 * inner_low + 3.0 * center) ** 2
    )
    rough_two = (
        13.0 / 12.0 * (inner_low - 2.0 * center + inner_high) ** 2
        + 0.25 * (inner_low - inner_high) ** 2
    )
    rough_three = (
        13.0 / 12.0 * (center - 2.0 * inner_high + outer_high) ** 2
        + 0.25 * (3.0 * center - 4.0 * inner_high + outer_high) ** 2
    )
    weight_one = 0.1 / (rough_one + epsilon) ** 2
    weight_two = 0.6 / (rough_two + epsilon) ** 2
    weight_three = 0.3 / (rough_three + epsilon) ** 2
    return (weight_one * guess_one + weight_two * guess_two + weight_three * guess_three) / (
        weight_one + weight_two + weight_three
    )


def weno_pair(padded, along, stride, length_of):
    differences = window_of(padded, 1, length_of + 5, along, stride) - window_of(
        padded, 0, length_of + 5, along, stride
    )
    stencil = [window_of(differences, shift_at, length_of, along, stride) for shift_at in range(6)]
    slope_minus = blend(stencil[0], stencil[1], stencil[2], stencil[3], stencil[4])
    slope_plus = blend(stencil[5], stencil[4], stencil[3], stencil[2], stencil[1])
    return (slope_minus, slope_plus)


def drift_tables(first_heading, count_h, total_h):
    heading_index = first_heading + jnp.arange(count_h, dtype=jnp.int32)
    heading_angle = heading_index.astype(jnp.float32) * (two_pi / total_h)
    speeds = 0.5 + jnp.arange(NV, dtype=jnp.int32).astype(jnp.float32) / (NV - 1)
    drift_x = (jnp.cos(heading_angle)[:, None] * speeds[None, :]).reshape(-1)
    drift_y = (jnp.sin(heading_angle)[:, None] * speeds[None, :]).reshape(-1)
    return (drift_x, drift_y)


def advance(level_set, padded_x, padded_y, padded_h, drift_x, drift_y):
    count_x = level_set.shape[0]
    count_y = level_set.shape[1]
    count_h = level_set.shape[2] // NV
    xm_slope, xp_slope = weno_pair(padded_x, 0, 1, count_x)
    ym_slope, yp_slope = weno_pair(padded_y, 1, 1, count_y)
    hm_slope, hp_slope = weno_pair(padded_h, 2, NV, count_h)
    hamiltonian = drift_x * (0.5 * (xm_slope + xp_slope)) + drift_y * (0.5 * (ym_slope + yp_slope))
    hamiltonian = hamiltonian - turn_rate * jnp.abs(0.5 * (hm_slope + hp_slope))
    hamiltonian = hamiltonian - 0.5 * (
        jnp.abs(drift_x) * (xp_slope - xm_slope)
        + jnp.abs(drift_y) * (yp_slope - ym_slope)
        + turn_rate * (hp_slope - hm_slope)
    )
    return level_set - time_step * jnp.maximum(hamiltonian, 0.0)


def read_corners(code_table, level_set):
    count_y = level_set.shape[1]
    plane_rows = level_set.shape[0] * count_y
    plane_columns = level_set.shape[2]
    grid_plane = level_set.reshape(plane_rows, plane_columns)
    slot_total = code_table.size
    block_size = math.gcd(slot_total, 128)
    clamped = jnp.maximum(code_table.reshape(-1), 0)
    row_start = (clamped // plane_columns).reshape(slot_total // block_size, block_size)
    column_start = (clamped % plane_columns).reshape(slot_total // block_size, block_size)
    row_offsets = jnp.array([0, 1, count_y, count_y + 1], dtype=jnp.int32)
    column_offsets = jnp.array([0, 1, NV, NV + 1], dtype=jnp.int32)
    row_iota = jnp.arange(plane_rows, dtype=jnp.int32)
    column_iota = jnp.arange(plane_columns, dtype=jnp.int32)

    def one_block(starts):
        row_index = starts[0][:, None] + row_offsets[None, :]
        selector = (row_index[:, :, None] == row_iota[None, None, :]).astype(jnp.float32)
        selector = selector.reshape(block_size * 4, plane_rows)
        picked = jnp.dot(
            selector,
            grid_plane,
            precision=lax.Precision.HIGHEST,
            preferred_element_type=jnp.float32,
        )
        picked = picked.reshape(block_size, 4, plane_columns)
        column_index = starts[1][:, None] + column_offsets[None, :]
        column_match = column_index[:, :, None] == column_iota[None, None, :]
        corner_read = jnp.sum(
            jnp.where(column_match[:, None, :, :], picked[:, :, None, :], 0.0), axis=-1
        )
        return corner_read.reshape(block_size, 16)

    blocks_read = lax.map(one_block, (row_start, column_start))
    return blocks_read.reshape(slot_total, 16).T.reshape((16,) + code_table.shape[1:])


def local(initial_value, corner, weights):
    count_x = initial_value.shape[0]
    count_y = initial_value.shape[1]
    count_h = initial_value.shape[2] // NV
    total_h = count_h * lax.axis_size("ha")
    drift_x, drift_y = drift_tables(lax.axis_index("ha") * count_h, count_h, total_h)
    level_set = initial_value
    for step_index in range(STEPS):
        plane = extended(level_set, (("gx", 0), ("gy", 1)), 3, False)
        padded_x = plane[:, 3 : 3 + count_y, :]
        padded_y = plane[3 : 3 + count_x, :, :]
        padded_h = extended(level_set, (("ha", 2),), 3 * NV, True)
        level_set = advance(level_set, padded_x, padded_y, padded_h, drift_x, drift_y)
    size_x = lax.axis_size("gx")
    size_yh = lax.axis_size("gy") * lax.axis_size("ha")
    slot_count = corner.shape[1]
    request = corner.reshape(1, slot_count, size_x, size_yh)
    weight_table = weights.reshape(16, slot_count, size_x, size_yh)
    live_slot = request >= 0
    in_codes, in_weights = (
        lax.all_to_all(
            lax.all_to_all(
                request.astype(jnp.float32), "gx", split_axis=2, concat_axis=2, tiled=True
            ),
            ("gy", "ha"),
            split_axis=3,
            concat_axis=3,
            tiled=True,
        ),
        lax.all_to_all(
            lax.all_to_all(weight_table, "gx", split_axis=2, concat_axis=2, tiled=True),
            ("gy", "ha"),
            split_axis=3,
            concat_axis=3,
            tiled=True,
        ),
    )
    fetched = read_corners(in_codes.astype(jnp.int32), level_set)
    owner_sum = jnp.sum(in_weights * fetched, axis=0, keepdims=True)
    weighted = lax.all_to_all(
        lax.all_to_all(owner_sum, "gx", split_axis=2, concat_axis=2, tiled=True),
        ("gy", "ha"),
        split_axis=3,
        concat_axis=3,
        tiled=True,
    )
    sampled = jnp.where(live_slot, weighted, 0.0).reshape(1, slot_count, size_x * size_yh)
    return (level_set, sampled)


def solution(mesh):
    return jax.shard_map(
        local,
        mesh=mesh,
        in_specs=(
            P("gx", "gy", "ha"),
            P(("gx", "gy", "ha"), None, None),
            P(("gx", "gy", "ha"), None, None, None),
        ),
        out_specs=(P("gx", "gy", "ha"), P(("gx", "gy", "ha"), None, None)),
        check_vma=False,
    )
```

profile of v0, /device:TPU:0, one launch (start us, length us, event | category | flops | bytes accessed | tf_op | source)
XLA Modules:
  0.0 224.4 jit_solution(18344994865052547849)
XLA Ops:
  12.6 5.5 %all-to-all-start.2 = ((f32[1,4,4,8]{3,1,0,2:T(4,128)}), f32[1,4,4,8]{3,1,0,2:T(4,128)S(1)}, u32[]{:S(2)}, u32[]{:S(2)}) async-start(f32[1,4,4,8]{3,1,0,2:T(4,128)} %copy.113), calls=%async_computation.2 | async-start | bytes 16384 | tf_op jit(solution)/shard_map/all_to_all | solution.py:159
  18.2 3.7 %all-to-all-done.2 = f32[1,4,4,8]{3,1,0,2:T(4,128)S(1)} async-done(((f32[1,4,4,8]{3,1,0,2:T(4,128)}), f32[1,4,4,8]{3,1,0,2:T(4,128)S(1)}, u32[]{:S(2)}, u32[]{:S(2)}) %all-to-all-start.2) | async-done | bytes 544 | tf_op jit(solution)/shard_map/all_to_all | solution.py:159
  22.6 4.0 %all-to-all-start.3 = ((f32[1,4,4,8]{2,1,0,3:T(4,128)}), f32[1,4,4,8]{2,1,0,3:T(4,128)S(1)}, u32[]{:S(2)}, u32[]{:S(2)}) async-start(f32[1,4,4,8]{2,1,0,3:T(4,128)} %copy.114), calls=%async_computation.3 | async-start | bytes 32768 | tf_op jit(solution)/shard_map/all_to_all | solution.py:158
  27.7 5.6 %all-to-all-done.3 = f32[1,4,4,8]{2,1,0,3:T(4,128)S(1)} async-done(((f32[1,4,4,8]{2,1,0,3:T(4,128)}), f32[1,4,4,8]{2,1,0,3:T(4,128)S(1)}, u32[]{:S(2)}, u32[]{:S(2)}) %all-to-all-start.3) | async-done | bytes 544 | tf_op jit(solution)/shard_map/all_to_all | solution.py:158
  33.2 3.2 %all-to-all-start = ((f32[4,1,512]{2,1,0:T(1,128)}), f32[4,1,512]{2,1,0:T(1,128)S(1)}, u32[]{:S(2)}, u32[]{:S(2)}) async-start(f32[4,1,512]{2,1,0:T(1,128)} %reshape.235), calls=%async_computation | async-start | bytes 16384 | tf_op jit(solution)/shard_map/all_to_all | solution.py:168
  37.6 2.7 %all-to-all-done = f32[4,1,512]{2,1,0:T(1,128)S(1)} async-done(((f32[4,1,512]{2,1,0:T(1,128)}), f32[4,1,512]{2,1,0:T(1,128)S(1)}, u32[]{:S(2)}, u32[]{:S(2)}) %all-to-all-start) | async-done | bytes 8224 | tf_op jit(solution)/shard_map/all_to_all | solution.py:168
  42.2 3.3 %all-to-all-start.1 = ((f32[8,1,256]{2,1,0:T(1,128)}), f32[8,1,256]{2,1,0:T(1,128)S(1)}, u32[]{:S(2)}, u32[]{:S(2)}) async-start(f32[8,1,256]{2,1,0:T(1,128)} %reshape.237), calls=%async_computation.1 | async-start | bytes 16384 | tf_op jit(solution)/shard_map/all_to_all | solution.py:167
  46.7 5.3 %all-to-all-done.1 = f32[8,1,256]{2,1,0:T(1,128)S(1)} async-done(((f32[8,1,256]{2,1,0:T(1,128)}), f32[8,1,256]{2,1,0:T(1,128)S(1)}, u32[]{:S(2)}, u32[]{:S(2)}) %all-to-all-start.1) | async-done | bytes 8224 | tf_op jit(solution)/shard_map/all_to_all | solution.py:167
  62.8 3.0 %collective-permute-done.3 = f32[22,3,1024]{2,0,1:T(8,128)} collective-permute-done((f32[22,3,1024]{2,0,1:T(8,128)S(1)}, f32[22,3,1024]{2,0,1:T(8,128)}, u32[]{:S(2)}, u32[]{:S(2)}) %collective-permute-start.3) | collective-permute-done | bytes 270368 | tf_op jit(solution)/shard_map/ppermute | solution.py:28
  67.6 14.8 %multiply_subtract_fusion.3 = f32[16,16,1024]{2,1,0:T(8,128)S(1)} fusion(f32[16,16,1024]{2,1,0:T(8,128)S(1)} %copy-done, f32[16,16,1344]{2,1,0:T(8,128)S(1)} %slice_subtract_fusion.7, f32[16,21,1024]{2,1,0:T(8,128)S(1)} %slice_subtract_fusion.3, f32[21,16,1024]{2,1,0:T(8,128)S(1)} %slice_subtract_fusion.11, f32[1024]{0:T(1024)S(1)} %abs.42, ...), kind=kLoop, calls=%fused_computation.24 | loop fusion | flops 103022592 | bytes 20987904 | tf_op jit(solution)/shard_map/sub | solution.py:98
  85.7 3.3 %collective-permute-start.11 = (f32[16,16,192]{2,1,0:T(8,128)S(1)}, f32[16,16,192]{2,1,0:T(8,128)}, u32[]{:S(2)}, u32[]{:S(2)}) collective-permute-start(f32[16,16,192]{2,1,0:T(8,128)S(1)} %get-tuple-element.49), channel_id=1, source_target_pairs={{1,0},{2,1},{3,2},{0,3},{5,4},{6,5},{7,6},{4,7},{9,8},{10,9},{11,1... | collective-permute-start | bytes 589832 | tf_op jit(solution)/shard_map/ppermute | solution.py:28
  90.2 3.0 %collective-permute-start.8 = (f32[22,3,1024]{2,0,1:T(8,128)}, f32[22,3,1024]{2,0,1:T(8,128)}, u32[]{:S(2)}, u32[]{:S(2)}) collective-permute-start(f32[22,3,1024]{2,0,1:T(8,128)} %copy.98), channel_id=1, source_target_pairs={{0,4},{1,5},{2,6},{3,7},{8,12},{9,13},{10,14},{11,15},{16,20},{17,... | collective-permute-start | bytes 811016 | tf_op jit(solution)/shard_map/ppermute | solution.py:26
  96.0 4.4 %collective-permute-done.11 = f32[16,16,192]{2,1,0:T(8,128)} collective-permute-done((f32[16,16,192]{2,1,0:T(8,128)S(1)}, f32[16,16,192]{2,1,0:T(8,128)}, u32[]{:S(2)}, u32[]{:S(2)}) %collective-permute-start.11) | collective-permute-done | bytes 196640 | tf_op jit(solution)/shard_map/ppermute | solution.py:28
  107.2 14.8 %multiply_subtract_fusion.2 = f32[16,16,1024]{2,1,0:T(8,128)S(1)} fusion(f32[16,16,1024]{2,1,0:T(8,128)S(1)} %multiply_subtract_fusion.3, f32[16,16,1344]{2,1,0:T(8,128)S(1)} %slice_subtract_fusion.6, f32[16,21,1024]{2,1,0:T(8,128)S(1)} %slice_subtract_fusion.2, f32[21,16,1024]{2,1,0:T(8,128)S(1)} %slice_subtract_fusion.10, f32[1024]{0:T(1024)S(1)} %abs.42, ...), kind=kLoop, calls=%fused_computation.23 | loop fusion | flops 103022592 | bytes 20987904 | tf_op jit(solution)/shard_map/sub | solution.py:98
  126.7 3.0 %collective-permute-start.17 = (f32[16,16,192]{2,1,0:T(8,128)S(1)}, f32[16,16,192]{2,1,0:T(8,128)}, u32[]{:S(2)}, u32[]{:S(2)}) collective-permute-start(f32[16,16,192]{2,1,0:T(8,128)S(1)} %get-tuple-element.45), channel_id=1, source_target_pairs={{1,0},{2,1},{3,2},{0,3},{5,4},{6,5},{7,6},{4,7},{9,8},{10,9},{11,1... | collective-permute-start | bytes 589832 | tf_op jit(solution)/shard_map/ppermute | solution.py:28
  136.8 4.6 %collective-permute-done.17 = f32[16,16,192]{2,1,0:T(8,128)} collective-permute-done((f32[16,16,192]{2,1,0:T(8,128)S(1)}, f32[16,16,192]{2,1,0:T(8,128)}, u32[]{:S(2)}, u32[]{:S(2)}) %collective-permute-start.17) | collective-permute-done | bytes 196640 | tf_op jit(solution)/shard_map/ppermute | solution.py:28
  148.0 14.8 %multiply_subtract_fusion.1 = f32[16,16,1024]{2,1,0:T(8,128)S(1)} fusion(f32[16,16,1024]{2,1,0:T(8,128)S(1)} %multiply_subtract_fusion.2, f32[16,16,1344]{2,1,0:T(8,128)S(1)} %slice_subtract_fusion.5, f32[16,21,1024]{2,1,0:T(8,128)S(1)} %slice_subtract_fusion.1, f32[21,16,1024]{2,1,0:T(8,128)S(1)} %slice_subtract_fusion.9, f32[1024]{0:T(1024)S(1)} %abs.42, ...), kind=kLoop, calls=%fused_computation.22 | loop fusion | flops 103022592 | bytes 20987904 | tf_op jit(solution)/shard_map/sub | solution.py:98
  167.8 2.6 %collective-permute-start.23 = (f32[16,16,192]{2,1,0:T(8,128)S(1)}, f32[16,16,192]{2,1,0:T(8,128)}, u32[]{:S(2)}, u32[]{:S(2)}) collective-permute-start(f32[16,16,192]{2,1,0:T(8,128)S(1)} %get-tuple-element.41), channel_id=1, source_target_pairs={{1,0},{2,1},{3,2},{0,3},{5,4},{6,5},{7,6},{4,7},{9,8},{10,9},{11,1... | collective-permute-start | bytes 589832 | tf_op jit(solution)/shard_map/ppermute | solution.py:28
  175.0 2.6 %collective-permute-done.22 = f32[16,16,192]{2,1,0:T(8,128)} collective-permute-done((f32[16,16,192]{2,1,0:T(8,128)S(1)}, f32[16,16,192]{2,1,0:T(8,128)}, u32[]{:S(2)}, u32[]{:S(2)}) %collective-permute-start.22) | collective-permute-done | bytes 196640 | tf_op jit(solution)/shard_map/ppermute | solution.py:26
  177.6 4.7 %collective-permute-done.23 = f32[16,16,192]{2,1,0:T(8,128)} collective-permute-done((f32[16,16,192]{2,1,0:T(8,128)S(1)}, f32[16,16,192]{2,1,0:T(8,128)}, u32[]{:S(2)}, u32[]{:S(2)}) %collective-permute-start.23) | collective-permute-done | bytes 196640 | tf_op jit(solution)/shard_map/ppermute | solution.py:28
  189.1 14.8 %multiply_subtract_fusion = f32[16,16,1024]{2,1,0:T(8,128)S(1)} fusion(f32[16,16,1024]{2,1,0:T(8,128)S(1)} %multiply_subtract_fusion.1, f32[16,16,1344]{2,1,0:T(8,128)S(1)} %slice_subtract_fusion.4, f32[16,21,1024]{2,1,0:T(8,128)S(1)} %slice_subtract_fusion, f32[21,16,1024]{2,1,0:T(8,128)S(1)} %slice_subtract_fusion.8, f32[1024]{0:T(1024)S(1)} %abs.42, ...), kind=kLoop, calls=%fused_computation.21 | loop fusion | flops 103022592 | bytes 20987904 | tf_op jit(solution)/shard_map/sub | solution.py:98
  206.8 6.2 %all_to_all.30 = f32[1,4,4,8]{3,1,0,2:T(4,128)S(1)} all-to-all(f32[1,4,4,8]{3,1,0,2:T(4,128)S(1)} %copy.118), channel_id=1, replica_groups=mesh['gx'=4,'gy'=2,'ha'=4] {'gx'}, dimensions={2} | all-to-all | bytes 1024 | tf_op jit(solution)/shard_map/all_to_all | solution.py:178
  213.7 3.4 %all-to-all-start.5 = ((f32[1,4,4,8]{2,1,0,3:T(4,128)}), f32[1,4,4,8]{2,1,0,3:T(4,128)S(1)}, u32[]{:S(2)}, u32[]{:S(2)}) async-start(f32[1,4,4,8]{2,1,0,3:T(4,128)} %copy.119), calls=%async_computation.5 | async-start | bytes 32768 | tf_op jit(solution)/shard_map/all_to_all | solution.py:177
  217.1 6.5 %all-to-all-done.5 = f32[1,4,4,8]{2,1,0,3:T(4,128)S(1)} async-done(((f32[1,4,4,8]{2,1,0,3:T(4,128)}), f32[1,4,4,8]{2,1,0,3:T(4,128)S(1)}, u32[]{:S(2)}, u32[]{:S(2)}) %all-to-all-start.5) | async-done | bytes 544 | tf_op jit(solution)/shard_map/all_to_all | solution.py:177
  (154 shorter events, 83.3 us)
Async XLA Ops:
  1.7 51.6 %collective-permute-start = (f32[3,16,1024]{2,1,0:T(8,128)S(1)}, f32[3,16,1024]{2,1,0:T(8,128)S(1)}, u32[]{:S(2)}, u32[]{:S(2)}) collective-permute-start(f32[3,16,1024]{2,1,0:T(8,128)S(1)} %get-tuple-element.52), channel_id=1, source_target_pairs={{0,8},{8,16},{16,24},{1,9},{9,17},{17,25},{2,10},{10,18},{18,26},{... | collective-permute-start | bytes 589832 | tf_op jit(solution)/shard_map/ppermute | solution.py:26
  4.1 49.4 %collective-permute-start.1 = (f32[3,16,1024]{2,1,0:T(8,128)S(1)}, f32[3,16,1024]{2,1,0:T(8,128)S(1)}, u32[]{:S(2)}, u32[]{:S(2)}) collective-permute-start(f32[3,16,1024]{2,1,0:T(8,128)S(1)} %get-tuple-element.51), channel_id=1, source_target_pairs={{8,0},{16,8},{24,16},{9,1},{17,9},{25,17},{10,2},{18,10},{26,18},{... | collective-permute-start | bytes 589832 | tf_op jit(solution)/shard_map/ppermute | solution.py:28
  7.5 50.4 %collective-permute-start.4 = (f32[16,16,192]{2,1,0:T(8,128)}, f32[16,16,192]{2,1,0:T(8,128)}, u32[]{:S(2)}, u32[]{:S(2)}) collective-permute-start(f32[16,16,192]{2,1,0:T(8,128)} %get-tuple-element.54), channel_id=1, source_target_pairs={{0,1},{1,2},{2,3},{3,0},{4,5},{5,6},{6,7},{7,4},{8,9},{9,10},{10,1... | collective-permute-start | bytes 589832 | tf_op jit(solution)/shard_map/ppermute | solution.py:26
  9.9 48.0 %collective-permute-start.5 = (f32[16,16,192]{2,1,0:T(8,128)}, f32[16,16,192]{2,1,0:T(8,128)}, u32[]{:S(2)}, u32[]{:S(2)}) collective-permute-start(f32[16,16,192]{2,1,0:T(8,128)} %get-tuple-element.53), channel_id=1, source_target_pairs={{1,0},{2,1},{3,2},{0,3},{5,4},{6,5},{7,6},{4,7},{9,8},{10,9},{11,1... | collective-permute-start | bytes 589832 | tf_op jit(solution)/shard_map/ppermute | solution.py:28
  12.6 9.3 %all-to-all-start.2 = ((f32[1,4,4,8]{3,1,0,2:T(4,128)}), f32[1,4,4,8]{3,1,0,2:T(4,128)S(1)}, u32[]{:S(2)}, u32[]{:S(2)}) async-start(f32[1,4,4,8]{3,1,0,2:T(4,128)} %copy.113), calls=%async_computation.2 | async-start | bytes 16384 | tf_op jit(solution)/shard_map/all_to_all | solution.py:159
  22.6 10.6 %all-to-all-start.3 = ((f32[1,4,4,8]{2,1,0,3:T(4,128)}), f32[1,4,4,8]{2,1,0,3:T(4,128)S(1)}, u32[]{:S(2)}, u32[]{:S(2)}) async-start(f32[1,4,4,8]{2,1,0,3:T(4,128)} %copy.114), calls=%async_computation.3 | async-start | bytes 32768 | tf_op jit(solution)/shard_map/all_to_all | solution.py:158
  42.2 9.8 %all-to-all-start.1 = ((f32[8,1,256]{2,1,0:T(1,128)}), f32[8,1,256]{2,1,0:T(1,128)S(1)}, u32[]{:S(2)}, u32[]{:S(2)}) async-start(f32[8,1,256]{2,1,0:T(1,128)} %reshape.237), calls=%async_computation.1 | async-start | bytes 16384 | tf_op jit(solution)/shard_map/all_to_all | solution.py:167
  53.9 8.7 %collective-permute-start.2 = (f32[22,3,1024]{2,0,1:T(8,128)S(1)}, f32[22,3,1024]{2,0,1:T(8,128)S(1)}, u32[]{:S(2)}, u32[]{:S(2)}) collective-permute-start(f32[22,3,1024]{2,0,1:T(8,128)S(1)} %copy.94), channel_id=1, source_target_pairs={{0,4},{1,5},{2,6},{3,7},{8,12},{9,13},{10,14},{11,15},{16,20},{17,... | collective-permute-start | bytes 811016 | tf_op jit(solution)/shard_map/ppermute | solution.py:26
  56.5 9.3 %collective-permute-start.3 = (f32[22,3,1024]{2,0,1:T(8,128)S(1)}, f32[22,3,1024]{2,0,1:T(8,128)}, u32[]{:S(2)}, u32[]{:S(2)}) collective-permute-start(f32[22,3,1024]{2,0,1:T(8,128)S(1)} %copy.95), channel_id=1, source_target_pairs={{4,0},{5,1},{6,2},{7,3},{12,8},{13,9},{14,10},{15,11},{20,16},{21,... | collective-permute-start | bytes 811016 | tf_op jit(solution)/shard_map/ppermute | solution.py:28
  85.2 10.9 %collective-permute-start.10 = (f32[16,16,192]{2,1,0:T(8,128)S(1)}, f32[16,16,192]{2,1,0:T(8,128)}, u32[]{:S(2)}, u32[]{:S(2)}) collective-permute-start(f32[16,16,192]{2,1,0:T(8,128)S(1)} %get-tuple-element.50), channel_id=1, source_target_pairs={{0,1},{1,2},{2,3},{3,0},{4,5},{5,6},{6,7},{7,4},{8,9},{9,10},{10,1... | collective-permute-start | bytes 589832 | tf_op jit(solution)/shard_map/ppermute | solution.py:26
  85.7 14.7 %collective-permute-start.11 = (f32[16,16,192]{2,1,0:T(8,128)S(1)}, f32[16,16,192]{2,1,0:T(8,128)}, u32[]{:S(2)}, u32[]{:S(2)}) collective-permute-start(f32[16,16,192]{2,1,0:T(8,128)S(1)} %get-tuple-element.49), channel_id=1, source_target_pairs={{1,0},{2,1},{3,2},{0,3},{5,4},{6,5},{7,6},{4,7},{9,8},{10,9},{11,1... | collective-permute-start | bytes 589832 | tf_op jit(solution)/shard_map/ppermute | solution.py:28
  90.2 14.9 %collective-permute-start.8 = (f32[22,3,1024]{2,0,1:T(8,128)}, f32[22,3,1024]{2,0,1:T(8,128)}, u32[]{:S(2)}, u32[]{:S(2)}) collective-permute-start(f32[22,3,1024]{2,0,1:T(8,128)} %copy.98), channel_id=1, source_target_pairs={{0,4},{1,5},{2,6},{3,7},{8,12},{9,13},{10,14},{11,15},{16,20},{17,... | collective-permute-start | bytes 811016 | tf_op jit(solution)/shard_map/ppermute | solution.py:26
  94.1 12.2 %collective-permute-start.9 = (f32[22,3,1024]{2,0,1:T(8,128)}, f32[22,3,1024]{2,0,1:T(8,128)S(1)}, u32[]{:S(2)}, u32[]{:S(2)}) collective-permute-start(f32[22,3,1024]{2,0,1:T(8,128)} %copy.99), channel_id=1, source_target_pairs={{4,0},{5,1},{6,2},{7,3},{12,8},{13,9},{14,10},{15,11},{20,16},{21,... | collective-permute-start | bytes 811016 | tf_op jit(solution)/shard_map/ppermute | solution.py:28
  122.0 7.6 %collective-permute-start.12 = (f32[3,16,1024]{2,1,0:T(8,128)S(1)}, f32[3,16,1024]{2,1,0:T(8,128)S(1)}, u32[]{:S(2)}, u32[]{:S(2)}) collective-permute-start(f32[3,16,1024]{2,1,0:T(8,128)S(1)} %get-tuple-element.43), channel_id=1, source_target_pairs={{0,8},{8,16},{16,24},{1,9},{9,17},{17,25},{2,10},{10,18},{18,26},{... | collective-permute-start | bytes 589832 | tf_op jit(solution)/shard_map/ppermute | solution.py:26
  125.6 11.2 %collective-permute-start.16 = (f32[16,16,192]{2,1,0:T(8,128)S(1)}, f32[16,16,192]{2,1,0:T(8,128)}, u32[]{:S(2)}, u32[]{:S(2)}) collective-permute-start(f32[16,16,192]{2,1,0:T(8,128)S(1)} %get-tuple-element.46), channel_id=1, source_target_pairs={{0,1},{1,2},{2,3},{3,0},{4,5},{5,6},{6,7},{7,4},{8,9},{9,10},{10,1... | collective-permute-start | bytes 589832 | tf_op jit(solution)/shard_map/ppermute | solution.py:26
  126.7 14.7 %collective-permute-start.17 = (f32[16,16,192]{2,1,0:T(8,128)S(1)}, f32[16,16,192]{2,1,0:T(8,128)}, u32[]{:S(2)}, u32[]{:S(2)}) collective-permute-start(f32[16,16,192]{2,1,0:T(8,128)S(1)} %get-tuple-element.45), channel_id=1, source_target_pairs={{1,0},{2,1},{3,2},{0,3},{5,4},{6,5},{7,6},{4,7},{9,8},{10,9},{11,1... | collective-permute-start | bytes 589832 | tf_op jit(solution)/shard_map/ppermute | solution.py:28
  130.1 15.9 %collective-permute-start.14 = (f32[22,3,1024]{2,0,1:T(8,128)S(1)}, f32[22,3,1024]{2,0,1:T(8,128)S(1)}, u32[]{:S(2)}, u32[]{:S(2)}) collective-permute-start(f32[22,3,1024]{2,0,1:T(8,128)S(1)} %copy.102), channel_id=1, source_target_pairs={{0,4},{1,5},{2,6},{3,7},{8,12},{9,13},{10,14},{11,15},{16,20},{17,... | collective-permute-start | bytes 811016 | tf_op jit(solution)/shard_map/ppermute | solution.py:26
  133.3 13.0 %collective-permute-start.15 = (f32[22,3,1024]{2,0,1:T(8,128)}, f32[22,3,1024]{2,0,1:T(8,128)}, u32[]{:S(2)}, u32[]{:S(2)}) collective-permute-start(f32[22,3,1024]{2,0,1:T(8,128)} %copy.103), channel_id=1, source_target_pairs={{4,0},{5,1},{6,2},{7,3},{12,8},{13,9},{14,10},{15,11},{20,16},{21,... | collective-permute-start | bytes 811016 | tf_op jit(solution)/shard_map/ppermute | solution.py:28
  162.9 7.6 %collective-permute-start.18 = (f32[3,16,1024]{2,1,0:T(8,128)S(1)}, f32[3,16,1024]{2,1,0:T(8,128)S(1)}, u32[]{:S(2)}, u32[]{:S(2)}) collective-permute-start(f32[3,16,1024]{2,1,0:T(8,128)S(1)} %get-tuple-element.39), channel_id=1, source_target_pairs={{0,8},{8,16},{16,24},{1,9},{9,17},{17,25},{2,10},{10,18},{18,26},{... | collective-permute-start | bytes 589832 | tf_op jit(solution)/shard_map/ppermute | solution.py:26
  166.6 11.0 %collective-permute-start.22 = (f32[16,16,192]{2,1,0:T(8,128)S(1)}, f32[16,16,192]{2,1,0:T(8,128)}, u32[]{:S(2)}, u32[]{:S(2)}) collective-permute-start(f32[16,16,192]{2,1,0:T(8,128)S(1)} %get-tuple-element.42), channel_id=1, source_target_pairs={{0,1},{1,2},{2,3},{3,0},{4,5},{5,6},{6,7},{7,4},{8,9},{9,10},{10,1... | collective-permute-start | bytes 589832 | tf_op jit(solution)/shard_map/ppermute | solution.py:26
  167.8 14.5 %collective-permute-start.23 = (f32[16,16,192]{2,1,0:T(8,128)S(1)}, f32[16,16,192]{2,1,0:T(8,128)}, u32[]{:S(2)}, u32[]{:S(2)}) collective-permute-start(f32[16,16,192]{2,1,0:T(8,128)S(1)} %get-tuple-element.41), channel_id=1, source_target_pairs={{1,0},{2,1},{3,2},{0,3},{5,4},{6,5},{7,6},{4,7},{9,8},{10,9},{11,1... | collective-permute-start | bytes 589832 | tf_op jit(solution)/shard_map/ppermute | solution.py:28
  171.0 16.1 %collective-permute-start.20 = (f32[22,3,1024]{2,0,1:T(8,128)S(1)}, f32[22,3,1024]{2,0,1:T(8,128)S(1)}, u32[]{:S(2)}, u32[]{:S(2)}) collective-permute-start(f32[22,3,1024]{2,0,1:T(8,128)S(1)} %copy.106), channel_id=1, source_target_pairs={{0,4},{1,5},{2,6},{3,7},{8,12},{9,13},{10,14},{11,15},{16,20},{17,... | collective-permute-start | bytes 811016 | tf_op jit(solution)/shard_map/ppermute | solution.py:26
  173.5 13.8 %collective-permute-start.21 = (f32[22,3,1024]{2,0,1:T(8,128)}, f32[22,3,1024]{2,0,1:T(8,128)}, u32[]{:S(2)}, u32[]{:S(2)}) collective-permute-start(f32[22,3,1024]{2,0,1:T(8,128)} %copy.107), channel_id=1, source_target_pairs={{4,0},{5,1},{6,2},{7,3},{12,8},{13,9},{14,10},{15,11},{20,16},{21,... | collective-permute-start | bytes 811016 | tf_op jit(solution)/shard_map/ppermute | solution.py:28
  213.7 10.0 %all-to-all-start.5 = ((f32[1,4,4,8]{2,1,0,3:T(4,128)}), f32[1,4,4,8]{2,1,0,3:T(4,128)S(1)}, u32[]{:S(2)}, u32[]{:S(2)}) async-start(f32[1,4,4,8]{2,1,0,3:T(4,128)} %copy.119), calls=%async_computation.5 | async-start | bytes 32768 | tf_op jit(solution)/shard_map/all_to_all | solution.py:177
  (15 other events, 210.7 us)
where the time goes:
time: 226 us; the launch traced here: 224 us
  other arithmetic  76 us (34%)
  starting transfers between devices  63.8 us (28%)
  waiting for transfers between devices  45.8 us (20%)
  local copies, waits for them, and re-layouts  30.1 us (13%)
  blocking collectives  6.18 us (3%)
    sub x4, other arithmetic, advance(): return level_set - time_step * jnp.maximum(hamiltonian, 0.0)  59.2 us
    ppermute x12, starting transfers between devices, extended(): lax.ppermute(tail, axis, [(i, (i + 1) % count) for i in range(ends)])  22.8 us
    ppermute x12, starting transfers between devices, extended(): lax.ppermute(head, axis, [((i + 1) % count, i) for i in range(ends)])  21.6 us
    ppermute x12, waiting for transfers between devices, extended(): lax.ppermute(head, axis, [((i + 1) % count, i) for i in range(ends)])  16.7 us
    sub x12, other arithmetic, weno_pair(): window_of(padded, 1, length_of + 5, along, stride)  10.3 us
    concatenate x5, local copies, waits for them, and re-layouts, extended(): jnp.concatenate([lax.ppermute(tail, axis, [(i, (i + 1) % count) for i in...  9.5 us
    all_to_all x1, waiting for transfers between devices, local(): lax.all_to_all(lax.all_to_all(owner_sum, 'gx', split_axis=2, concat_axis=...  6.49 us
    all_to_all x1, blocking collectives, local(): lax.all_to_all(owner_sum, 'gx', split_axis=2, concat_axis=2, tiled=True)  6.18 us
  transfers between devices with their start and end apart: 29, of which 12 were waited for; matrix products, arithmetic and copies ran while one was open for 16% of the time, Pallas kernels for 0%

commit v1 on v0

v1 whole, which is shorter than its diff:
```python
import functools

import jax
import jax.numpy as jnp
import numpy as np
from jax import lax
from jax.experimental import pallas as pl
from jax.experimental.pallas import tpu as pltpu
from jax.sharding import PartitionSpec as P

NV = 64
STEPS = 4
CAP = 4
MESH = pl.DeviceIdType.MESH
EPS4 = 4e-6
DT = 0.15
LO, HI = 3, 2


def smooth(t):
    return (13.0 / 3.0) * (t * t) + EPS4


def square(v):
    return v * v


def upwind_line(cells):
    n = len(cells)
    d = [cells[i + 1] - cells[i] for i in range(n - 1)]
    e = [d[i + 1] - d[i] for i in range(n - 2)]
    t = [e[i + 1] - e[i] for i in range(n - 3)]
    z = [t[i] - t[i + 1] for i in range(n - 4)]
    m = [smooth(v) for v in t]
    e3 = [3.0 * v for v in e]
    out = []
    for i in range(n - 5):
        s1 = square(m[i] + square(e3[i + 1] - e[i]))
        s2 = square(m[i + 1] + square(e[i + 1] + e[i + 2]))
        s3 = square(m[i + 2] + square(e3[i + 2] - e[i + 3]))
        bc = s2 * s3
        ab = 3.0 * (s1 * s2)
        w = bc + ab + 6.0 * (s1 * s3)
        num = (z[i] + z[i]) * bc + z[i + 1] * ab
        lin = 6.0 * d[i + 2] + (e[i + 1] + (e[i + 2] + e[i + 2]))
        out.append(lin + num * pl.reciprocal(w, approx=True))
    return out


def heading_term(u):
    d = [u[i + 1] - u[i] for i in range(6)]
    e = [d[i + 1] - d[i] for i in range(5)]
    t = [e[i + 1] - e[i] for i in range(4)]
    z = [t[i] - t[i + 1] for i in range(3)]
    m = [smooth(v) for v in t]
    e3 = [3.0 * v for v in e]

    def parts(i):
        s1 = square(m[i] + square(e3[i + 1] - e[i]))
        s2 = square(m[i + 1] + square(e[i + 1] + e[i + 2]))
        s3 = square(m[i + 2] + square(e3[i + 2] - e[i + 3]))
        return s1 * s2, s2 * s3, 6.0 * (s1 * s3)

    ab, bc, ac = parts(0)
    ab = 3.0 * ab
    num = (z[0] + z[0]) * bc + z[1] * ab
    minus = 6.0 * d[2] + (e[1] + (e[2] + e[2])) + num * pl.reciprocal(bc + ab + ac, approx=True)
    ab, bc, ac = parts(1)
    bc = 3.0 * bc
    num = (z[2] + z[2]) * ab + z[1] * bc
    negated = (e[3] + (e[2] + e[2])) - 6.0 * d[3] + num * pl.reciprocal(bc + ab + ac, approx=True)
    return jnp.minimum(minus, negated)


def kernel(sizes, v_hbm, code_ref, wt_ref, drift_ref, out_hbm, res_ref,
           grid, hxy, stage, send_h, recv_h, code_in, wt_in, code_s, wt_s, rows,
           in_sem, out_sem, halo_send, halo_recv, cs_sem, cr_sem, ws_sem, wr_sem, rs_sem, rr_sem, loc_sem):
    ngx, ngy, nha, cx, cy, nj = sizes
    total = ngx * ngy * nha
    gx, gy, ha = lax.axis_index("gx"), lax.axis_index("gy"), lax.axis_index("ha")
    me = (gx * ngy + gy) * nha + ha
    quarter = ha * 4 // nha
    east = (quarter == 0) | (quarter == 3)
    north = quarter < 2
    sx = jnp.where(east, 1, -1)
    sy = jnp.where(north, 1, -1)
    x0 = jnp.where(east, 0, cx - 1)
    y0 = jnp.where(north, 0, cy - 1)
    xb = jnp.where(east, 0, cx + 2 * LO - 1)
    yb = jnp.where(north, 0, cy + 2 * LO - 1)

    def near(forward, a, b, count):
        return pl.ds(jnp.where(forward, a, b), count)

    def up_dst(forward, c):
        return near(forward, 0, c + LO, LO)

    def up_src(forward, c):
        return near(forward, c, LO, LO)

    def down_dst(forward, c):
        return near(forward, c + LO, LO - HI, HI)

    def down_src(forward, c):
        return near(forward, LO, c + LO - HI, HI)


    def device_of(o):
        return (o // (ngy * nha), (o // nha) % ngy, o % nha)

    loads = [
        pltpu.make_async_copy(
            v_hbm.at[:, pl.ds(128 * j, 128)], stage.at[pl.ds(j * cx * cy, cx * cy)], in_sem.at[j])
        for j in range(nj)
    ]
    for c in loads:
        c.start()

    barrier = pltpu.get_barrier_semaphore()

    @pl.loop(1, total)
    def _(i):
        pl.semaphore_signal(barrier, inc=1, device_id=device_of((me + i) % total), device_id_type=MESH)

    tile0 = jnp.zeros((8, 128), jnp.float32)
    x_up = gx - sx
    x_down = gx + sx
    y_up = gy - sy
    y_down = gy + sy
    has_xu = (x_up >= 0) & (x_up < ngx)
    has_xd = (x_down >= 0) & (x_down < ngx)
    has_yu = (y_up >= 0) & (y_up < ngy)
    has_yd = (y_down >= 0) & (y_down < ngy)

    def zero_x(first, count):
        @pl.loop(0, STEPS)
        def _(n):
            @pl.loop(0, cy)
            def _(y):
                for x in range(count):
                    grid[n, y + LO, first + x, 8:16, :] = tile0

    def zero_y(first, count):
        @pl.loop(0, STEPS)
        def _(n):
            @pl.loop(0, cx)
            def _(x):
                for y in range(count):
                    grid[n, first + y, x + LO, 8:16, :] = tile0

    pl.when(jnp.logical_not(has_xu))(lambda: zero_x(jnp.where(east, 0, cx + LO), LO))
    pl.when(jnp.logical_not(has_xd))(lambda: zero_x(jnp.where(east, cx + LO, LO - HI), HI))
    pl.when(jnp.logical_not(has_yu))(lambda: zero_y(jnp.where(north, 0, cy + LO), LO))
    pl.when(jnp.logical_not(has_yd))(lambda: zero_y(jnp.where(north, cy + LO, LO - HI), HI))

    for c in loads:
        c.wait()

    @pl.loop(0, cy)
    def _(y):
        for x in range(cx):
            row = x * cy + y
            grid[0, y + LO, x + LO, 8:16, :] = stage[pl.ds(row, nj, stride=cx * cy), :]

    pl.semaphore_wait(barrier, total - 1)

    def request(o):
        return (
            pltpu.make_async_remote_copy(
                src_ref=code_ref.at[o], dst_ref=code_in.at[me], send_sem=cs_sem.at[o],
                recv_sem=cr_sem.at[me], device_id=device_of(o), device_id_type=MESH),
            pltpu.make_async_remote_copy(
                src_ref=wt_ref.at[o], dst_ref=wt_in.at[me], send_sem=ws_sem.at[o],
                recv_sem=wr_sem.at[me], device_id=device_of(o), device_id_type=MESH),
        )

    def request_from(o):
        return (
            pltpu.make_async_remote_copy(
                src_ref=code_ref.at[o], dst_ref=code_in.at[o], send_sem=cs_sem.at[o],
                recv_sem=cr_sem.at[o], device_id=device_of(o), device_id_type=MESH),
            pltpu.make_async_remote_copy(
                src_ref=wt_ref.at[o], dst_ref=wt_in.at[o], send_sem=ws_sem.at[o],
                recv_sem=wr_sem.at[o], device_id=device_of(o), device_id_type=MESH),
        )

    ys, xs = pl.ds(LO, cy), pl.ds(LO, cx)

    def x_copies(n):
        g = grid.at[n]
        up = pltpu.make_async_remote_copy(
            src_ref=g.at[ys, up_src(east, cx), pl.ds(8, 8)], dst_ref=g.at[ys, up_dst(east, cx), pl.ds(8, 8)],
            send_sem=halo_send.at[n, 0], recv_sem=halo_recv.at[n, 0],
            device_id=(x_down, gy, ha), device_id_type=MESH)
        down = pltpu.make_async_remote_copy(
            src_ref=g.at[ys, down_src(east, cx), pl.ds(8, 8)], dst_ref=g.at[ys, down_dst(east, cx), pl.ds(8, 8)],
            send_sem=halo_send.at[n, 1], recv_sem=halo_recv.at[n, 1],
            device_id=(x_up, gy, ha), device_id_type=MESH)
        return up, down

    def y_copies(n):
        g = grid.at[n]
        up = pltpu.make_async_remote_copy(
            src_ref=g.at[up_src(north, cy), xs, pl.ds(8, 8)], dst_ref=g.at[up_dst(north, cy), xs, pl.ds(8, 8)],
            send_sem=halo_send.at[n, 2], recv_sem=halo_recv.at[n, 2],
            device_id=(gx, y_down, ha), device_id_type=MESH)
        down = pltpu.make_async_remote_copy(
            src_ref=g.at[down_src(north, cy), xs, pl.ds(8, 8)], dst_ref=g.at[down_dst(north, cy), xs, pl.ds(8, 8)],
            send_sem=halo_send.at[n, 3], recv_sem=halo_recv.at[n, 3],
            device_id=(gx, y_up, ha), device_id_type=MESH)
        return up, down

    def h_copies(n):
        return tuple(
            pltpu.make_async_remote_copy(
                src_ref=send_h.at[n, k], dst_ref=recv_h.at[n, k],
                send_sem=halo_send.at[n, 4 + k], recv_sem=halo_recv.at[n, 4 + k],
                device_id=(gx, gy, (ha + (1 if k == 0 else nha - 1)) % nha), device_id_type=MESH)
            for k in range(2))

    low_half = lax.broadcasted_iota(jnp.int32, (8, 128), 1) < NV

    def swap(v):
        return pltpu.roll(v, NV, 1)

    flat = grid.reshape(grid.shape[0] * grid.shape[1] * grid.shape[2] * 24, 128)

    def row_of(n, y, x, r):
        return ((n * (cy + 2 * LO) + y + LO) * (cx + 2 * LO) + x + LO) * 24 + r

    halves = cx // 16

    def send(n):
        @pl.loop(0, cy)
        def _(y):
            for q in range(2 * halves):
                send_h[n, 0, y * 2 * halves + q] = flat[pl.ds(row_of(n, y, 8 * q, 15), 8, stride=24), :]
                send_h[n, 1, y * 2 * halves + q] = flat[pl.ds(row_of(n, y, 8 * q, 8), 8, stride=24), :]
            for q in range(halves):
                a = flat[pl.ds(row_of(n, y, 16 * q, 14), 8, stride=24), :]
                b = flat[pl.ds(row_of(n, y, 16 * q + 8, 14), 8, stride=24), :]
                send_h[n, 0, cy * 2 * halves + y * halves + q] = jnp.where(low_half, swap(a), b)
                a = flat[pl.ds(row_of(n, y, 16 * q, 9), 8, stride=24), :]
                b = flat[pl.ds(row_of(n, y, 16 * q + 8, 9), 8, stride=24), :]
                send_h[n, 1, cy * 2 * halves + y * halves + q] = jnp.where(low_half, a, swap(b))

        for c in h_copies(n):
            c.start()
        xu, xd = x_copies(n)
        yu, yd = y_copies(n)
        pl.when(has_yd)(lambda: yu.start())
        pl.when(has_yu)(lambda: yd.start())
        pl.when(has_xd)(lambda: xu.start())
        pl.when(has_xu)(lambda: xd.start())

    def unpack(n):
        @pl.loop(0, cy)
        def _(y):
            for q in range(2 * halves):
                flat[pl.ds(row_of(n, y, 8 * q, 7), 8, stride=24), :] = recv_h[n, 0, y * 2 * halves + q]
                flat[pl.ds(row_of(n, y, 8 * q, 16), 8, stride=24), :] = recv_h[n, 1, y * 2 * halves + q]
            for q in range(halves):
                v = recv_h[n, 0, cy * 2 * halves + y * halves + q]
                flat[pl.ds(row_of(n, y, 16 * q, 6), 8, stride=24), :] = swap(v)
                flat[pl.ds(row_of(n, y, 16 * q + 8, 6), 8, stride=24), :] = v
                v = recv_h[n, 1, cy * 2 * halves + y * halves + q]
                flat[pl.ds(row_of(n, y, 16 * q, 17), 8, stride=24), :] = v
                flat[pl.ds(row_of(n, y, 16 * q + 8, 17), 8, stride=24), :] = swap(v)

    send(0)

    @pl.loop(1, total)
    def _(i):
        for c in request((me + i) % total):
            c.start()

    own = (pltpu.make_async_copy(code_ref.at[me], code_in.at[me], loc_sem.at[0]),
           pltpu.make_async_copy(wt_ref.at[me], wt_in.at[me], loc_sem.at[1]))
    for c in own:
        c.start()
    for c in own:
        c.wait()

    drift_x = drift_ref[ha, 0]
    drift_y = drift_ref[ha, 1]

    @pl.loop(0, STEPS)
    def _(n):
        yu, yd = y_copies(n)
        pl.when(has_yu)(lambda: yu.wait_recv())
        pl.when(has_yd)(lambda: yd.wait_recv())

        @pl.loop(0, cx)
        def _(x):
            line = upwind_line([grid[n, yb + sy * i, x + LO, 8:16, :] for i in range(LO + cy + HI)])
            for y in range(cy):
                hxy[y0 + sy * y, x] = drift_y * line[y]

        xu, xd = x_copies(n)
        pl.when(has_xu)(lambda: xu.wait_recv())
        pl.when(has_xd)(lambda: xd.wait_recv())

        @pl.loop(0, cy)
        def _(y):
            line = upwind_line([grid[n, y + LO, xb + sx * i, 8:16, :] for i in range(LO + cx + HI)])
            for x in range(cx):
                hxy[y, x0 + sx * x] += drift_x * line[x]

        for c in h_copies(n):
            c.wait_recv()
        unpack(n)

        @pl.loop(0, cy)
        def _(y):
            for x in range(cx):
                g = [grid[n, y + LO, x + LO, pl.ds(r, 8), :] for r in range(6, 11)]
                s = [swap(v) for v in g]
                odd = [jnp.where(low_half, s[i], s[i + 1]) for i in range(4)]
                term = heading_term([odd[0], g[1], odd[1], g[2], odd[2], g[3], odd[3]])
                ham = hxy[y, x] + (DT / 6.0) * term
                grid[n + 1, y + LO, x + LO, 8:16, :] = g[2] - jnp.maximum(ham, 0.0)

        pl.when(n < STEPS - 1)(lambda: send(n + 1))

    @pl.loop(0, cy)
    def _(y):
        for x in range(cx):
            row = x * cy + y
            stage[pl.ds(row, nj, stride=cx * cy), :] = grid[STEPS, y + LO, x + LO, 8:16, :]

    stores = [
        pltpu.make_async_copy(
            stage.at[pl.ds(j * cx * cy, cx * cy)], out_hbm.at[:, pl.ds(128 * j, 128)], out_sem.at[j])
        for j in range(nj)
    ]
    for c in stores:
        c.start()

    @pl.loop(1, total)
    def _(i):
        for c in request_from((me + i) % total):
            c.wait()

    to_s = (pltpu.make_async_copy(code_in, code_s, loc_sem.at[0]),
            pltpu.make_async_copy(wt_in, wt_s, loc_sem.at[1]))
    for c in to_s:
        c.start()
    for c in to_s:
        c.wait()

    ramp = (lax.broadcasted_iota(jnp.int32, (8, 128), 0) * 128
            + lax.broadcasted_iota(jnp.int32, (8, 128), 1))
    hv = nj * 128

    def answer(o, slot_of):
        return pltpu.make_async_remote_copy(
            src_ref=rows.at[o], dst_ref=res_ref.at[slot_of], send_sem=rs_sem.at[o],
            recv_sem=rr_sem.at[slot_of], device_id=device_of(o), device_id_type=MESH)

    @pl.loop(0, total)
    def _(i):
        o = (me + i + 1) % total
        for slot in range(CAP):
            c = jnp.maximum(code_s[o, 0, slot], 0)
            a = c // (cy * hv)
            b = (c // hv) % cy
            at = ramp - c % hv
            hits = [at == off for off in (0, 1, NV, NV + 1)]
            acc = None
            for i1 in range(2):
                for i2 in range(2):
                    w = jnp.zeros((8, 128), jnp.float32)
                    for k in range(4):
                        w = jnp.where(hits[k], wt_s[o, 0, slot * 16 + 8 * i1 + 4 * i2 + k], w)
                    part = w * grid[STEPS, b + i2 + LO, a + i1 + LO, 8:16, :]
                    acc = part if acc is None else acc + part
            rows[o, slot:slot + 1, :] = jnp.sum(acc, axis=0, keepdims=True)
        pl.when(o != me)(lambda: answer(o, me).start())

    mine = pltpu.make_async_copy(rows.at[me], res_ref.at[me], loc_sem.at[2])
    mine.start()
    mine.wait()

    @pl.loop(1, total)
    def _(i):
        o = (me + i) % total
        answer(o, o).wait()

    @pl.loop(0, STEPS)
    def _(n):
        xu, xd = x_copies(n)
        yu, yd = y_copies(n)
        pl.when(has_yd)(lambda: yu.wait_send())
        pl.when(has_yu)(lambda: yd.wait_send())
        pl.when(has_xd)(lambda: xu.wait_send())
        pl.when(has_xu)(lambda: xd.wait_send())
        for c in h_copies(n):
            c.wait_send()

    for c in stores:
        c.wait()


def drift_table(nha, ch, nj):
    heads = nha * ch
    angle = np.arange(heads, dtype=np.int32).astype(np.float32) * np.float32(6.283185307179586 / heads)
    speed = np.float32(0.5) + np.arange(NV, dtype=np.float32) / np.float32(NV - 1)
    quarter = np.arange(heads) * 4 // heads
    sign_x = np.where((quarter == 0) | (quarter == 3), 1.0, -1.0).astype(np.float32)
    sign_y = np.where(quarter < 2, 1.0, -1.0).astype(np.float32)
    table = np.stack([(sign_x * np.cos(angle))[:, None] * speed, (sign_y * np.sin(angle))[:, None] * speed])
    table = table * np.float32(DT / 6.0)
    return table.reshape(2, nha, nj, 128).transpose(1, 0, 2, 3).astype(np.float32)


def solution(mesh):
    ngx, ngy, nha = (mesh.shape[k] for k in ("gx", "gy", "ha"))
    total = ngx * ngy * nha
    assert nha % 4 == 0

    def local(initial_value, corner, weights):
        cx, cy, chv = initial_value.shape
        nj = chv // 128
        assert nj == 8 and cx % 16 == 0
        table = jnp.asarray(drift_table(nha, chv // NV, nj))
        codes = jnp.pad(corner[0].T, ((0, 0), (0, 128 - CAP))).reshape(total, 1, 128)
        wts = weights[0].transpose(2, 1, 0).reshape(total, CAP * 16)
        wts = jnp.pad(wts, ((0, 0), (0, 128 - CAP * 16))).reshape(total, 1, 128)
        f32, i32 = jnp.float32, jnp.int32
        tiles = cy * (cx // 16) * 3
        dma = pltpu.SemaphoreType.DMA
        vmem = pl.BlockSpec(memory_space=pltpu.VMEM)
        any_ = pl.BlockSpec(memory_space=pl.ANY)
        final, parts = pl.pallas_call(
            functools.partial(kernel, (ngx, ngy, nha, cx, cy, nj)),
            out_shape=(jax.ShapeDtypeStruct((cx * cy, chv), f32),
                       jax.ShapeDtypeStruct((total, CAP, 128), f32)),
            in_specs=[any_, vmem, vmem, vmem],
            out_specs=(any_, vmem),
            scratch_shapes=[
                pltpu.VMEM((STEPS + 1, cy + 2 * LO, cx + 2 * LO, 24, 128), f32),
                pltpu.VMEM((cy, cx, 8, 128), f32),
                pltpu.VMEM((nj * cx * cy, 128), f32),
                pltpu.VMEM((STEPS, 2, tiles, 8, 128), f32),
                pltpu.VMEM((STEPS, 2, tiles, 8, 128), f32),
                pltpu.VMEM((total, 1, 128), i32),
                pltpu.VMEM((total, 1, 128), f32),
                pltpu.SMEM((total, 1, 128), i32),
                pltpu.SMEM((total, 1, 128), f32),
                pltpu.VMEM((total, CAP, 128), f32),
                dma((nj,)), dma((nj,)), dma((STEPS, 6)), dma((STEPS, 6)),
                dma((total,)), dma((total,)), dma((total,)), dma((total,)),
                dma((total,)), dma((total,)), dma((3,)),
            ],
            compiler_params=pltpu.CompilerParams(
                collective_id=0, has_side_effects=True, vmem_limit_bytes=56 * 1024 * 1024),
        )(initial_value.reshape(cx * cy, chv), codes, wts, table)
        sampled = jnp.sum(parts, axis=2).T[None]
        return (final.reshape(cx, cy, chv), jnp.where(corner >= 0, sampled, 0.0))

    return jax.shard_map(
        local,
        mesh=mesh,
        in_specs=(P("gx", "gy", "ha"), P(("gx", "gy", "ha"), None, None),
                  P(("gx", "gy", "ha"), None, None, None)),
        out_specs=(P("gx", "gy", "ha"), P(("gx", "gy", "ha"), None, None)),
        check_vma=False,
    )
```

time: 226 us -> 95.1 us (0.42)
  Pallas kernels: 0 us -> 87.5 us
  other arithmetic: 76 us -> 1.53 us
  starting transfers between devices: 63.8 us -> 0 us
  waiting for transfers between devices: 45.8 us -> 0 us
  local copies, waits for them, and re-layouts: 30.1 us -> 5.05 us
  blocking collectives: 6.18 us -> 0 us
    pallas_call x0 -> x1, Pallas kernels: none -> 87.5 us  [local(): pl.pallas_call(functools.partial(kernel, (ngx, ngy, nha, cx, cy, nj)), ou...]
    sub x16 -> x0, other arithmetic: 69.6 us -> none  [the longest x4 59.2 us: advance(): return level_set - time_step * jnp.maximum(hamiltonian, 0.0)]
    ppermute x24 -> x0, starting transfers between devices: 44.3 us -> none  [the longest x12 22.8 us: extended(): lax.ppermute(tail, axis, [(i, (i + 1) % count) for i in range(ends)])]
    all_to_all x5 -> x0, waiting for transfers between devices: 23.7 us -> none  [the longest x1 6.49 us: local(): lax.all_to_all(lax.all_to_all(owner_sum, 'gx', split_axis=2, concat_axis=...]
    ppermute x24 -> x0, waiting for transfers between devices: 22.2 us -> none  [the longest x12 16.7 us: extended(): lax.ppermute(head, axis, [((i + 1) % count, i) for i in range(ends)])]
    all_to_all x5 -> x0, starting transfers between devices: 19.5 us -> none  [the longest x1 5.5 us: local(): lax.all_to_all(request.astype(jnp.float32), 'gx', split_axis=2, concat_ax...]
    concatenate x5 -> x0, local copies, waits for them, and re-layouts: 9.5 us -> none  [extended(): jnp.concatenate([lax.ppermute(tail, axis, [(i, (i + 1) % count) for i in...]
    slice x20 -> x0, local copies, waits for them, and re-layouts: 8.19 us -> none  [the longest x9 6.13 us: extended(): head = lax.slice_in_dim(cells, 0, width, axis=dim)]
  transfers between devices with their start and end apart: 29 -> 0, of which waited for: 12 -> 0; matrix products, arithmetic and copies ran while one was open for 16% -> 0% of each run, Pallas kernels for 0% -> 0%
where the time goes in v1:
time: 95.1 us; the launch traced here: 94.7 us
  Pallas kernels  87.5 us (92%)
  local copies, waits for them, and re-layouts  5.05 us (5%)
  other arithmetic  1.53 us (2%)
    pallas_call x1, Pallas kernels, local(): pl.pallas_call(functools.partial(kernel, (ngx, ngy, nha, cx, cy, nj)), ou...  87.5 us
    unnamed x5, local copies, waits for them, and re-layouts  2.91 us

profile of v1, /device:TPU:0, one launch (start us, length us, event | category | flops | bytes accessed | tf_op | source)
XLA Modules:
  0.0 94.7 jit_solution(11562521151560303484)
XLA Ops:
  0.6 0.0 copy-start
  0.6 0.8 copy.11
  1.4 0.6 pad.8
  2.0 0.0 copy-done
  2.0 0.1 copy.13
  2.1 0.6 pad.9
  2.7 87.5 %shard_map.59 = (f32[256,1024]{1,0:T(8,128)}, f32[32,4,128]{2,1,0:T(4,128)}) custom-call(f32[256,1024]{1,0:T(8,128)} %bitcast.13, s32[32,1,128]{2,1,0:T(1,128)} %bitcast.16, f32[32,1,128]{2,1,0:T(1,128)} %bitcast.17, f32[4,2,8,128]{3,2,1,0:T(8,128)} %constant.8.clone.drift_ref), custom_call_target="tpu_custom_call" | custom-call | tf_op jit(solution)/shard_map/pallas_call | solution.py:434
  90.2 0.9 reduce_sum.9
  91.2 0.0 copy-start.1
  91.2 0.1 copy.14
  91.3 0.6 copy-done.1
  91.9 0.6 bitcast_select_fusion
  92.4 2.3 %copy.16 = f32[16,16,1024]{2,1,0:T(8,128)} copy(f32[16,16,1024]{2,1,0:T(8,128)} %bitcast.14) | data formatting | bytes 2097152
  (1 shorter events, 0.0 us)
Async XLA Ops:
  0.6 1.4 %copy-start = (f32[1,16,4,32]{3,2,1,0:T(4,128)S(1)}, f32[1,16,4,32]{3,2,1,0:T(4,128)}, u32[]{:S(2)}) copy-start(f32[1,16,4,32]{3,2,1,0:T(4,128)} %param.6) | copy-start | bytes 24580
  91.2 0.7 copy-start.1

commit v2 on v1

--- a/solution.py
+++ b/solution.py
@@ -15,6 +15,7 @@
 EPS4 = 4e-6
 DT = 0.15
 LO, HI = 3, 2
+CHUNKS = 4
 
 
 def smooth(t):
@@ -73,7 +74,7 @@
 
 
 def kernel(sizes, v_hbm, code_ref, wt_ref, drift_ref, out_hbm, res_ref,
-           grid, hxy, stage, send_h, recv_h, code_in, wt_in, code_s, wt_s, rows,
+           grid, hx, hy, stage, send_h, recv_h, code_in, wt_in, code_s, wt_s, rows,
            in_sem, out_sem, halo_send, halo_recv, cs_sem, cr_sem, ws_sem, wr_sem, rs_sem, rr_sem, loc_sem):
     ngx, ngy, nha, cx, cy, nj = sizes
     total = ngx * ngy * nha
@@ -210,11 +211,11 @@
             device_id=(gx, y_up, ha), device_id_type=MESH)
         return up, down
 
-    def h_copies(n):
+    def h_copies(n, c):
         return tuple(
             pltpu.make_async_remote_copy(
-                src_ref=send_h.at[n, k], dst_ref=recv_h.at[n, k],
-                send_sem=halo_send.at[n, 4 + k], recv_sem=halo_recv.at[n, 4 + k],
+                src_ref=send_h.at[n, k, c], dst_ref=recv_h.at[n, k, c],
+                send_sem=halo_send.at[n, 4 + k * CHUNKS + c], recv_sem=halo_recv.at[n, 4 + k * CHUNKS + c],
                 device_id=(gx, gy, (ha + (1 if k == 0 else nha - 1)) % nha), device_id_type=MESH)
             for k in range(2))
 
@@ -229,45 +230,65 @@
         return ((n * (cy + 2 * LO) + y + LO) * (cx + 2 * LO) + x + LO) * 24 + r
 
     halves = cx // 16
-
-    def send(n):
-        @pl.loop(0, cy)
-        def _(y):
-            for q in range(2 * halves):
-                send_h[n, 0, y * 2 * halves + q] = flat[pl.ds(row_of(n, y, 8 * q, 15), 8, stride=24), :]
-                send_h[n, 1, y * 2 * halves + q] = flat[pl.ds(row_of(n, y, 8 * q, 8), 8, stride=24), :]
-            for q in range(halves):
-                a = flat[pl.ds(row_of(n, y, 16 * q, 14), 8, stride=24), :]
-                b = flat[pl.ds(row_of(n, y, 16 * q + 8, 14), 8, stride=24), :]
-                send_h[n, 0, cy * 2 * halves + y * halves + q] = jnp.where(low_half, swap(a), b)
-                a = flat[pl.ds(row_of(n, y, 16 * q, 9), 8, stride=24), :]
-                b = flat[pl.ds(row_of(n, y, 16 * q + 8, 9), 8, stride=24), :]
-                send_h[n, 1, cy * 2 * halves + y * halves + q] = jnp.where(low_half, a, swap(b))
-
-        for c in h_copies(n):
-            c.start()
-        xu, xd = x_copies(n)
+    depth = cy // CHUNKS
+
+    def pack(n, c, r):
+        y = c * depth + r
+        for q in range(2 * halves):
+            send_h[n, 0, c, r * 2 * halves + q] = flat[pl.ds(row_of(n, y, 8 * q, 15), 8, stride=24), :]
+            send_h[n, 1, c, r * 2 * halves + q] = flat[pl.ds(row_of(n, y, 8 * q, 8), 8, stride=24), :]
+        for q in range(halves):
+            at = (2 * depth + r) * halves + q
+            a = flat[pl.ds(row_of(n, y, 16 * q, 14), 8, stride=24), :]
+            b = flat[pl.ds(row_of(n, y, 16 * q + 8, 14), 8, stride=24), :]
+            send_h[n, 0, c, at] = jnp.where(low_half, swap(a), b)
+            a = flat[pl.ds(row_of(n, y, 16 * q, 9), 8, stride=24), :]
+            b = flat[pl.ds(row_of(n, y, 16 * q + 8, 9), 8, stride=24), :]
+            send_h[n, 1, c, at] = jnp.where(low_half, a, swap(b))
+
+    def unpack(n, c, r):
+        y = c * depth + r
+        for q in range(2 * halves):
+            flat[pl.ds(row_of(n, y, 8 * q, 7), 8, stride=24), :] = recv_h[n, 0, c, r * 2 * halves + q]
+            flat[pl.ds(row_of(n, y, 8 * q, 16), 8, stride=24), :] = recv_h[n, 1, c, r * 2 * halves + q]
+        for q in range(halves):
+            at = (2 * depth + r) * halves + q
+            v = recv_h[n, 0, c, at]
+            flat[pl.ds(row_of(n, y, 16 * q, 6), 8, stride=24), :] = swap(v)
+            flat[pl.ds(row_of(n, y, 16 * q + 8, 6), 8, stride=24), :] = v
+            v = recv_h[n, 1, c, at]
+            flat[pl.ds(row_of(n, y, 16 * q, 17), 8, stride=24), :] = v
+            flat[pl.ds(row_of(n, y, 16 * q + 8, 17), 8, stride=24), :] = swap(v)
+
+    def send_chunk(n, c):
+        for copy in h_copies(n, c):
+            copy.start()
+
+    def send_y(n):
         yu, yd = y_copies(n)
         pl.when(has_yd)(lambda: yu.start())
         pl.when(has_yu)(lambda: yd.start())
+
+    def send_x(n):
+        xu, xd = x_copies(n)
         pl.when(has_xd)(lambda: xu.start())
         pl.when(has_xu)(lambda: xd.start())
 
-    def unpack(n):
-        @pl.loop(0, cy)
-        def _(y):
-            for q in range(2 * halves):
-                flat[pl.ds(row_of(n, y, 8 * q, 7), 8, stride=24), :] = recv_h[n, 0, y * 2 * halves + q]
-                flat[pl.ds(row_of(n, y, 8 * q, 16), 8, stride=24), :] = recv_h[n, 1, y * 2 * halves + q]
-            for q in range(halves):
-                v = recv_h[n, 0, cy * 2 * halves + y * halves + q]
-                flat[pl.ds(row_of(n, y, 16 * q, 6), 8, stride=24), :] = swap(v)
-                flat[pl.ds(row_of(n, y, 16 * q + 8, 6), 8, stride=24), :] = v
-                v = recv_h[n, 1, cy * 2 * halves + y * halves + q]
-                flat[pl.ds(row_of(n, y, 16 * q, 17), 8, stride=24), :] = v
-                flat[pl.ds(row_of(n, y, 16 * q + 8, 17), 8, stride=24), :] = swap(v)
-
-    send(0)
+    def chunk_at(i):
+        return (i + CHUNKS - 1) % CHUNKS
+
+    send_y(0)
+    send_x(0)
+
+    @pl.loop(0, CHUNKS)
+    def _(i):
+        c = chunk_at(i)
+
+        @pl.loop(0, depth)
+        def _(r):
+            pack(0, c, r)
+
+        send_chunk(0, c)
 
     @pl.loop(1, total)
     def _(i):
@@ -284,43 +305,60 @@
     drift_x = drift_ref[ha, 0]
     drift_y = drift_ref[ha, 1]
 
+    def y_part(n, first, count):
+        @pl.loop(0, cx)
+        def _(x):
+            line = upwind_line([grid[n, yb + sy * i, x + LO, 8:16, :] for i in range(first, first + count + 5)])
+            for k in range(count):
+                hy[y0 + sy * (first + k), x] = drift_y * line[k]
+
+    def x_part(n, first, count):
+        @pl.loop(0, cy)
+        def _(y):
+            line = upwind_line([grid[n, y + LO, xb + sx * i, 8:16, :] for i in range(first, first + count + 5)])
+            for k in range(count):
+                hx[y, x0 + sx * (first + k)] = drift_x * line[k]
+
     @pl.loop(0, STEPS)
     def _(n):
+        y_part(n, LO, cy - LO - HI)
+        x_part(n, LO, cx - LO - HI)
+
         yu, yd = y_copies(n)
         pl.when(has_yu)(lambda: yu.wait_recv())
         pl.when(has_yd)(lambda: yd.wait_recv())
-
-        @pl.loop(0, cx)
-        def _(x):
-            line = upwind_line([grid[n, yb + sy * i, x + LO, 8:16, :] for i in range(LO + cy + HI)])
-            for y in range(cy):
-                hxy[y0 + sy * y, x] = drift_y * line[y]
+        y_part(n, 0, LO)
+        y_part(n, cy - HI, HI)
 
         xu, xd = x_copies(n)
         pl.when(has_xu)(lambda: xu.wait_recv())
         pl.when(has_xd)(lambda: xd.wait_recv())
-
-        @pl.loop(0, cy)
-        def _(y):
-            line = upwind_line([grid[n, y + LO, xb + sx * i, 8:16, :] for i in range(LO + cx + HI)])
-            for x in range(cx):
-                hxy[y, x0 + sx * x] += drift_x * line[x]
-
-        for c in h_copies(n):
-            c.wait_recv()
-        unpack(n)
-
-        @pl.loop(0, cy)
-        def _(y):
-            for x in range(cx):
-                g = [grid[n, y + LO, x + LO, pl.ds(r, 8), :] for r in range(6, 11)]
-                s = [swap(v) for v in g]
-                odd = [jnp.where(low_half, s[i], s[i + 1]) for i in range(4)]
-                term = heading_term([odd[0], g[1], odd[1], g[2], odd[2], g[3], odd[3]])
-                ham = hxy[y, x] + (DT / 6.0) * term
-                grid[n + 1, y + LO, x + LO, 8:16, :] = g[2] - jnp.maximum(ham, 0.0)
-
-        pl.when(n < STEPS - 1)(lambda: send(n + 1))
+        x_part(n, 0, LO)
+        x_part(n, cx - HI, HI)
+
+        @pl.loop(0, CHUNKS)
+        def _(i):
+            c = chunk_at(i)
+            for copy in h_copies(n, c):
+                copy.wait_recv()
+
+            @pl.loop(0, depth)
+            def _(r):
+                y = c * depth + r
+                unpack(n, c, r)
+                for x in range(cx):
+                    g = [grid[n, y + LO, x + LO, pl.ds(r, 8), :] for r in range(6, 11)]
+                    s = [swap(v) for v in g]
+                    odd = [jnp.where(low_half, s[i], s[i + 1]) for i in range(4)]
+                    term = heading_term([odd[0], g[1], odd[1], g[2], odd[2], g[3], odd[3]])
+                    ham = hx[y, x] + hy[y, x] + (DT / 6.0) * term
+                    grid[n + 1, y + LO, x + LO, 8:16, :] = g[2] - jnp.maximum(ham, 0.0)
+                pl.when(n < STEPS - 1)(lambda: pack(n + 1, c, r))
+
+            pl.when(n < STEPS - 1)(lambda: send_chunk(n + 1, c))
+            pl.when((n < STEPS - 1) & (i == 1))(lambda: send_y(n + 1))
+
+        pl.when(n < STEPS - 1)(lambda: send_x(n + 1))
 
     @pl.loop(0, cy)
     def _(y):
@@ -394,8 +432,9 @@
         pl.when(has_yu)(lambda: yd.wait_send())
         pl.when(has_xd)(lambda: xu.wait_send())
         pl.when(has_xu)(lambda: xd.wait_send())
-        for c in h_copies(n):
-            c.wait_send()
+        for c in range(CHUNKS):
+            for copy in h_copies(n, c):
+                copy.wait_send()
 
     for c in stores:
         c.wait()
@@ -440,15 +479,16 @@
             scratch_shapes=[
                 pltpu.VMEM((STEPS + 1, cy + 2 * LO, cx + 2 * LO, 24, 128), f32),
                 pltpu.VMEM((cy, cx, 8, 128), f32),
+                pltpu.VMEM((cy, cx, 8, 128), f32),
                 pltpu.VMEM((nj * cx * cy, 128), f32),
-                pltpu.VMEM((STEPS, 2, tiles, 8, 128), f32),
-                pltpu.VMEM((STEPS, 2, tiles, 8, 128), f32),
+                pltpu.VMEM((STEPS, 2, CHUNKS, tiles // CHUNKS, 8, 128), f32),
+                pltpu.VMEM((STEPS, 2, CHUNKS, tiles // CHUNKS, 8, 128), f32),
                 pltpu.VMEM((total, 1, 128), i32),
                 pltpu.VMEM((total, 1, 128), f32),
                 pltpu.SMEM((total, 1, 128), i32),
                 pltpu.SMEM((total, 1, 128), f32),
                 pltpu.VMEM((total, CAP, 128), f32),
-                dma((nj,)), dma((nj,)), dma((STEPS, 6)), dma((STEPS, 6)),
+                dma((nj,)), dma((nj,)), dma((STEPS, 4 + 2 * CHUNKS)), dma((STEPS, 4 + 2 * CHUNKS)),
                 dma((total,)), dma((total,)), dma((total,)), dma((total,)),
                 dma((total,)), dma((total,)), dma((3,)),
             ],

time: 95.1 us -> 77.8 us (0.82)
  Pallas kernels: 87.5 us -> 70.2 us
    pallas_call x1, Pallas kernels: 87.5 us -> 70.2 us  [local(): pl.pallas_call(functools.partial(kernel, (ngx, ngy, nha, cx, cy, nj)), ou...]
where the time goes in v2:
time: 77.8 us; the launch traced here: 77.5 us
  Pallas kernels  70.2 us (90%)
  local copies, waits for them, and re-layouts  5.05 us (6%)
  other arithmetic  1.53 us (2%)
    pallas_call x1, Pallas kernels, local(): pl.pallas_call(functools.partial(kernel, (ngx, ngy, nha, cx, cy, nj)), ou...  70.2 us
    unnamed x5, local copies, waits for them, and re-layouts  2.91 us

profile of v2, /device:TPU:0, one launch (start us, length us, event | category | flops | bytes accessed | tf_op | source)
XLA Modules:
  0.0 77.5 jit_solution(7905794961117800660)
XLA Ops:
  0.6 0.0 copy-start
  0.6 0.8 copy.11
  1.4 0.6 pad.8
  2.0 0.0 copy-done
  2.0 0.1 copy.13
  2.1 0.6 pad.9
  2.7 70.2 %shard_map.59 = (f32[256,1024]{1,0:T(8,128)}, f32[32,4,128]{2,1,0:T(4,128)}) custom-call(f32[256,1024]{1,0:T(8,128)} %bitcast.13, s32[32,1,128]{2,1,0:T(1,128)} %bitcast.16, f32[32,1,128]{2,1,0:T(1,128)} %bitcast.17, f32[4,2,8,128]{3,2,1,0:T(8,128)} %constant.8.clone.drift_ref), custom_call_target="tpu_custom_call" | custom-call | tf_op jit(solution)/shard_map/pallas_call | solution.py:473
  72.9 0.9 %reduce_sum.9 = f32[32,4]{1,0:T(8,128)S(1)} reduce(f32[32,4,128]{2,1,0:T(4,128)} %get-tuple-element.5, f32[]{:T(128)} %constant.2.clone.1), dimensions={2}, to_apply=%region_0.1 | reduce | flops 16256 | bytes 66052 | tf_op jit(solution)/shard_map/reduce_sum | solution.py:498
  73.9 0.0 copy-start.1
  73.9 0.1 copy.14
  74.0 0.6 copy-done.1
  74.6 0.6 bitcast_select_fusion
  75.2 2.3 %copy.16 = f32[16,16,1024]{2,1,0:T(8,128)} copy(f32[16,16,1024]{2,1,0:T(8,128)} %bitcast.14) | data formatting | bytes 2097152
  (1 shorter events, 0.0 us)
Async XLA Ops:
  0.6 1.4 %copy-start = (f32[1,16,4,32]{3,2,1,0:T(4,128)S(1)}, f32[1,16,4,32]{3,2,1,0:T(4,128)}, u32[]{:S(2)}) copy-start(f32[1,16,4,32]{3,2,1,0:T(4,128)} %param.6) | copy-start | bytes 24580
  73.9 0.7 copy-start.1

commit v3 on v2

--- a/solution.py
+++ b/solution.py
@@ -22,11 +22,12 @@
     return (13.0 / 3.0) * (t * t) + EPS4
 
 
-def square(v):
+def weight(v):
+    v = pl.reciprocal(v, approx=True)
     return v * v
 
 
-def upwind_line(cells):
+def terms(cells):
     n = len(cells)
     d = [cells[i + 1] - cells[i] for i in range(n - 1)]
     e = [d[i + 1] - d[i] for i in range(n - 2)]
@@ -34,47 +35,42 @@
     z = [t[i] - t[i + 1] for i in range(n - 4)]
     m = [smooth(v) for v in t]
     e3 = [3.0 * v for v in e]
+    return d, e, z, m, e3
+
+
+def weights_at(i, e, m, e3):
+    u1 = e3[i + 1] - e[i]
+    u2 = e[i + 1] + e[i + 2]
+    u3 = e3[i + 2] - e[i + 3]
+    return weight(m[i] + u1 * u1), 6.0 * weight(m[i + 1] + u2 * u2), weight(m[i + 2] + u3 * u3)
+
+
+def upwind_line(cells):
+    d, e, z, m, e3 = terms(cells)
     out = []
-    for i in range(n - 5):
-        s1 = square(m[i] + square(e3[i + 1] - e[i]))
-        s2 = square(m[i + 1] + square(e[i + 1] + e[i + 2]))
-        s3 = square(m[i + 2] + square(e3[i + 2] - e[i + 3]))
-        bc = s2 * s3
-        ab = 3.0 * (s1 * s2)
-        w = bc + ab + 6.0 * (s1 * s3)
-        num = (z[i] + z[i]) * bc + z[i + 1] * ab
+    for i in range(len(cells) - 5):
+        g1, g2, g3 = weights_at(i, e, m, e3)
+        g3 = 3.0 * g3
+        num = (z[i] + z[i]) * g1 + z[i + 1] * g3
         lin = 6.0 * d[i + 2] + (e[i + 1] + (e[i + 2] + e[i + 2]))
-        out.append(lin + num * pl.reciprocal(w, approx=True))
+        out.append(lin + num * pl.reciprocal(g1 + g2 + g3, approx=True))
     return out
 
 
-def heading_term(u):
-    d = [u[i + 1] - u[i] for i in range(6)]
-    e = [d[i + 1] - d[i] for i in range(5)]
-    t = [e[i + 1] - e[i] for i in range(4)]
-    z = [t[i] - t[i + 1] for i in range(3)]
-    m = [smooth(v) for v in t]
-    e3 = [3.0 * v for v in e]
-
-    def parts(i):
-        s1 = square(m[i] + square(e3[i + 1] - e[i]))
-        s2 = square(m[i + 1] + square(e[i + 1] + e[i + 2]))
-        s3 = square(m[i + 2] + square(e3[i + 2] - e[i + 3]))
-        return s1 * s2, s2 * s3, 6.0 * (s1 * s3)
-
-    ab, bc, ac = parts(0)
-    ab = 3.0 * ab
-    num = (z[0] + z[0]) * bc + z[1] * ab
-    minus = 6.0 * d[2] + (e[1] + (e[2] + e[2])) + num * pl.reciprocal(bc + ab + ac, approx=True)
-    ab, bc, ac = parts(1)
-    bc = 3.0 * bc
-    num = (z[2] + z[2]) * ab + z[1] * bc
-    negated = (e[3] + (e[2] + e[2])) - 6.0 * d[3] + num * pl.reciprocal(bc + ab + ac, approx=True)
-    return jnp.minimum(minus, negated)
+def both_ways(cells):
+    d, e, z, m, e3 = terms(cells)
+    g1, g2, g3 = weights_at(0, e, m, e3)
+    c = 6.0 * d[2]
+    h1, h3 = 3.0 * g1, 3.0 * g3
+    forward = (c + (e[1] + (e[2] + e[2]))
+               + ((z[0] + z[0]) * g1 + z[1] * h3) * pl.reciprocal(g1 + g2 + h3, approx=True))
+    negated = ((e[2] + (e[1] + e[1])) - c
+               + ((z[1] + z[1]) * g3 + z[0] * h1) * pl.reciprocal(h1 + g2 + g3, approx=True))
+    return forward, negated
 
 
 def kernel(sizes, v_hbm, code_ref, wt_ref, drift_ref, out_hbm, res_ref,
-           grid, hx, hy, stage, send_h, recv_h, code_in, wt_in, code_s, wt_s, rows,
+           grid, hx, hy, moved, stage, send_h, recv_h, code_in, wt_in, code_s, wt_s, rows,
            in_sem, out_sem, halo_send, halo_recv, cs_sem, cr_sem, ws_sem, wr_sem, rs_sem, rr_sem, loc_sem):
     ngx, ngy, nha, cx, cy, nj = sizes
     total = ngx * ngy * nha
@@ -226,6 +222,8 @@
 
     flat = grid.reshape(grid.shape[0] * grid.shape[1] * grid.shape[2] * 24, 128)
 
+    moved_flat = moved.reshape(cx * 24, 128)
+
     def row_of(n, y, x, r):
         return ((n * (cy + 2 * LO) + y + LO) * (cx + 2 * LO) + x + LO) * 24 + r
 
@@ -254,8 +252,16 @@
         for q in range(halves):
             at = (2 * depth + r) * halves + q
             v = recv_h[n, 0, c, at]
-            flat[pl.ds(row_of(n, y, 16 * q, 6), 8, stride=24), :] = swap(v)
-            flat[pl.ds(row_of(n, y, 16 * q + 8, 6), 8, stride=24), :] = v
+            here = [send_h[n, 1, c, r * 2 * halves + 2 * q + k] for k in range(2)]
+            past = [recv_h[n, 0, c, r * 2 * halves + 2 * q + k] for k in range(2)]
+            edge, _ = both_ways([
+                v,
+                jnp.where(low_half, past[0], swap(past[1])), jnp.where(low_half, swap(past[0]), past[1]),
+                jnp.where(low_half, here[0], swap(here[1])), jnp.where(low_half, swap(here[0]), here[1]),
+                send_h[n, 1, c, at],
+            ])
+            moved_flat[pl.ds(16 * q * 24 + 7, 8, stride=24), :] = edge
+            moved_flat[pl.ds((16 * q + 8) * 24 + 7, 8, stride=24), :] = swap(edge)
             v = recv_h[n, 1, c, at]
             flat[pl.ds(row_of(n, y, 16 * q, 17), 8, stride=24), :] = v
             flat[pl.ds(row_of(n, y, 16 * q + 8, 17), 8, stride=24), :] = swap(v)
@@ -347,12 +353,16 @@
                 y = c * depth + r
                 unpack(n, c, r)
                 for x in range(cx):
-                    g = [grid[n, y + LO, x + LO, pl.ds(r, 8), :] for r in range(6, 11)]
+                    g = [grid[n, y + LO, x + LO, pl.ds(k, 8), :] for k in range(7, 11)]
                     s = [swap(v) for v in g]
-                    odd = [jnp.where(low_half, s[i], s[i + 1]) for i in range(4)]
-                    term = heading_term([odd[0], g[1], odd[1], g[2], odd[2], g[3], odd[3]])
+                    odd = [jnp.where(low_half, s[k], s[k + 1]) for k in range(3)]
+                    forward, negated = both_ways([g[0], odd[0], g[1], odd[1], g[2], odd[2]])
+                    forward = swap(forward)
+                    moved[x, 8:16, :] = forward
+                    forward = jnp.where(low_half, moved[x, 7:15, :], forward)
+                    term = jnp.minimum(forward, negated)
                     ham = hx[y, x] + hy[y, x] + (DT / 6.0) * term
-                    grid[n + 1, y + LO, x + LO, 8:16, :] = g[2] - jnp.maximum(ham, 0.0)
+                    grid[n + 1, y + LO, x + LO, 8:16, :] = g[1] - jnp.maximum(ham, 0.0)
                 pl.when(n < STEPS - 1)(lambda: pack(n + 1, c, r))
 
             pl.when(n < STEPS - 1)(lambda: send_chunk(n + 1, c))
@@ -480,6 +490,7 @@
                 pltpu.VMEM((STEPS + 1, cy + 2 * LO, cx + 2 * LO, 24, 128), f32),
                 pltpu.VMEM((cy, cx, 8, 128), f32),
                 pltpu.VMEM((cy, cx, 8, 128), f32),
+                pltpu.VMEM((cx, 24, 128), f32),
                 pltpu.VMEM((nj * cx * cy, 128), f32),
                 pltpu.VMEM((STEPS, 2, CHUNKS, tiles // CHUNKS, 8, 128), f32),
                 pltpu.VMEM((STEPS, 2, CHUNKS, tiles // CHUNKS, 8, 128), f32),

time: 77.8 us -> 78.1 us (level)
  no operation moved by 1% of the time
where the time goes in v3:
time: 78.1 us; the launch traced here: 77.7 us
  Pallas kernels  70.5 us (90%)
  local copies, waits for them, and re-layouts  5.05 us (6%)
  other arithmetic  1.53 us (2%)
    pallas_call x1, Pallas kernels, local(): pl.pallas_call(functools.partial(kernel, (ngx, ngy, nha, cx, cy, nj)), ou...  70.5 us
    unnamed x5, local copies, waits for them, and re-layouts  2.91 us

profile of v3, /device:TPU:0, one launch (start us, length us, event | category | flops | bytes accessed | tf_op | source)
XLA Modules:
  0.0 77.7 jit_solution(6671436864370831507)
XLA Ops:
  0.6 0.0 copy-start
  0.6 0.8 copy.11
  1.4 0.6 pad.8
  2.0 0.0 copy-done
  2.0 0.1 copy.13
  2.1 0.6 pad.9
  2.7 70.5 %shard_map.59 = (f32[256,1024]{1,0:T(8,128)}, f32[32,4,128]{2,1,0:T(4,128)}) custom-call(f32[256,1024]{1,0:T(8,128)} %bitcast.13, s32[32,1,128]{2,1,0:T(1,128)} %bitcast.16, f32[32,1,128]{2,1,0:T(1,128)} %bitcast.17, f32[4,2,8,128]{3,2,1,0:T(8,128)} %constant.8.clone.drift_ref), custom_call_target="tpu_custom_call" | custom-call | tf_op jit(solution)/shard_map/pallas_call | solution.py:483
  73.2 0.9 %reduce_sum.9 = f32[32,4]{1,0:T(8,128)S(1)} reduce(f32[32,4,128]{2,1,0:T(4,128)} %get-tuple-element.5, f32[]{:T(128)} %constant.2.clone.1), dimensions={2}, to_apply=%region_0.1 | reduce | flops 16256 | bytes 66052 | tf_op jit(solution)/shard_map/reduce_sum | solution.py:509
  74.2 0.0 copy-start.1
  74.2 0.1 copy.14
  74.2 0.6 copy-done.1
  74.8 0.6 bitcast_select_fusion
  75.4 2.3 %copy.16 = f32[16,16,1024]{2,1,0:T(8,128)} copy(f32[16,16,1024]{2,1,0:T(8,128)} %bitcast.14) | data formatting | bytes 2097152
  (1 shorter events, 0.0 us)
Async XLA Ops:
  0.6 1.4 %copy-start = (f32[1,16,4,32]{3,2,1,0:T(4,128)S(1)}, f32[1,16,4,32]{3,2,1,0:T(4,128)}, u32[]{:S(2)}) copy-start(f32[1,16,4,32]{3,2,1,0:T(4,128)} %param.6) | copy-start | bytes 24580
  74.2 0.7 copy-start.1

commit v4 on v3

--- a/solution.py
+++ b/solution.py
@@ -181,17 +181,19 @@
                 recv_sem=wr_sem.at[o], device_id=device_of(o), device_id_type=MESH),
         )
 
-    ys, xs = pl.ds(LO, cy), pl.ds(LO, cx)
-
-    def x_copies(n):
+    xs = pl.ds(LO, cx)
+    depth = cy // CHUNKS
+
+    def x_copies(n, c):
         g = grid.at[n]
+        ys = pl.ds(LO + c * depth, depth)
         up = pltpu.make_async_remote_copy(
             src_ref=g.at[ys, up_src(east, cx), pl.ds(8, 8)], dst_ref=g.at[ys, up_dst(east, cx), pl.ds(8, 8)],
-            send_sem=halo_send.at[n, 0], recv_sem=halo_recv.at[n, 0],
+            send_sem=halo_send.at[n, 2 + c], recv_sem=halo_recv.at[n, 2 + c],
             device_id=(x_down, gy, ha), device_id_type=MESH)
         down = pltpu.make_async_remote_copy(
             src_ref=g.at[ys, down_src(east, cx), pl.ds(8, 8)], dst_ref=g.at[ys, down_dst(east, cx), pl.ds(8, 8)],
-            send_sem=halo_send.at[n, 1], recv_sem=halo_recv.at[n, 1],
+            send_sem=halo_send.at[n, 2 + CHUNKS + c], recv_sem=halo_recv.at[n, 2 + CHUNKS + c],
             device_id=(x_up, gy, ha), device_id_type=MESH)
         return up, down
 
@@ -199,11 +201,11 @@
         g = grid.at[n]
         up = pltpu.make_async_remote_copy(
             src_ref=g.at[up_src(north, cy), xs, pl.ds(8, 8)], dst_ref=g.at[up_dst(north, cy), xs, pl.ds(8, 8)],
-            send_sem=halo_send.at[n, 2], recv_sem=halo_recv.at[n, 2],
+            send_sem=halo_send.at[n, 0], recv_sem=halo_recv.at[n, 0],
             device_id=(gx, y_down, ha), device_id_type=MESH)
         down = pltpu.make_async_remote_copy(
             src_ref=g.at[down_src(north, cy), xs, pl.ds(8, 8)], dst_ref=g.at[down_dst(north, cy), xs, pl.ds(8, 8)],
-            send_sem=halo_send.at[n, 3], recv_sem=halo_recv.at[n, 3],
+            send_sem=halo_send.at[n, 1], recv_sem=halo_recv.at[n, 1],
             device_id=(gx, y_up, ha), device_id_type=MESH)
         return up, down
 
@@ -211,7 +213,7 @@
         return tuple(
             pltpu.make_async_remote_copy(
                 src_ref=send_h.at[n, k, c], dst_ref=recv_h.at[n, k, c],
-                send_sem=halo_send.at[n, 4 + k * CHUNKS + c], recv_sem=halo_recv.at[n, 4 + k * CHUNKS + c],
+                send_sem=halo_send.at[n, 2 + (2 + k) * CHUNKS + c], recv_sem=halo_recv.at[n, 2 + (2 + k) * CHUNKS + c],
                 device_id=(gx, gy, (ha + (1 if k == 0 else nha - 1)) % nha), device_id_type=MESH)
             for k in range(2))
 
@@ -228,7 +230,6 @@
         return ((n * (cy + 2 * LO) + y + LO) * (cx + 2 * LO) + x + LO) * 24 + r
 
     halves = cx // 16
-    depth = cy // CHUNKS
 
     def pack(n, c, r):
         y = c * depth + r
@@ -270,21 +271,22 @@
         for copy in h_copies(n, c):
             copy.start()
 
-    def send_y(n):
+    def send_y(n, low):
         yu, yd = y_copies(n)
-        pl.when(has_yd)(lambda: yu.start())
-        pl.when(has_yu)(lambda: yd.start())
-
-    def send_x(n):
-        xu, xd = x_copies(n)
+        up = jnp.logical_not(north) if low else north
+        pl.when(up & has_yd)(lambda: yu.start())
+        pl.when(jnp.logical_not(up) & has_yu)(lambda: yd.start())
+
+    def send_x(n, c):
+        xu, xd = x_copies(n, c)
         pl.when(has_xd)(lambda: xu.start())
         pl.when(has_xu)(lambda: xd.start())
 
     def chunk_at(i):
-        return (i + CHUNKS - 1) % CHUNKS
-
-    send_y(0)
-    send_x(0)
+        return jnp.where(i < 2, i + 1, jnp.where(i == 2, 0, 3))
+
+    send_y(0, True)
+    send_y(0, False)
 
     @pl.loop(0, CHUNKS)
     def _(i):
@@ -295,6 +297,7 @@
             pack(0, c, r)
 
         send_chunk(0, c)
+        send_x(0, c)
 
     @pl.loop(1, total)
     def _(i):
@@ -314,37 +317,31 @@
     def y_part(n, first, count):
         @pl.loop(0, cx)
         def _(x):
-            line = upwind_line([grid[n, yb + sy * i, x + LO, 8:16, :] for i in range(first, first + count + 5)])
+            line = upwind_line([grid[n, yb + sy * (first + i), x + LO, 8:16, :] for i in range(count + 5)])
             for k in range(count):
                 hy[y0 + sy * (first + k), x] = drift_y * line[k]
 
-    def x_part(n, first, count):
-        @pl.loop(0, cy)
-        def _(y):
-            line = upwind_line([grid[n, y + LO, xb + sx * i, 8:16, :] for i in range(first, first + count + 5)])
-            for k in range(count):
-                hx[y, x0 + sx * (first + k)] = drift_x * line[k]
+    def x_part(n, c):
+        @pl.loop(0, depth)
+        def _(r):
+            y = c * depth + r
+            line = upwind_line([grid[n, y + LO, xb + sx * i, 8:16, :] for i in range(cx + 5)])
+            for k in range(cx):
+                hx[y, x0 + sx * k] = drift_x * line[k]
 
     @pl.loop(0, STEPS)
     def _(n):
-        y_part(n, LO, cy - LO - HI)
-        x_part(n, LO, cx - LO - HI)
-
-        yu, yd = y_copies(n)
-        pl.when(has_yu)(lambda: yu.wait_recv())
-        pl.when(has_yd)(lambda: yd.wait_recv())
-        y_part(n, 0, LO)
-        y_part(n, cy - HI, HI)
-
-        xu, xd = x_copies(n)
-        pl.when(has_xu)(lambda: xu.wait_recv())
-        pl.when(has_xd)(lambda: xd.wait_recv())
-        x_part(n, 0, LO)
-        x_part(n, cx - HI, HI)
-
         @pl.loop(0, CHUNKS)
         def _(i):
             c = chunk_at(i)
+            yu, yd = y_copies(n)
+            pl.when((i == 2) & has_yu)(lambda: yu.wait_recv())
+            pl.when((i == 2) & has_yd)(lambda: yd.wait_recv())
+            y_part(n, depth * jnp.where(north, c, CHUNKS - 1 - c), depth)
+            xu, xd = x_copies(n, c)
+            pl.when(has_xu)(lambda: xu.wait_recv())
+            pl.when(has_xd)(lambda: xd.wait_recv())
+            x_part(n, c)
             for copy in h_copies(n, c):
                 copy.wait_recv()
 
@@ -365,10 +362,12 @@
                     grid[n + 1, y + LO, x + LO, 8:16, :] = g[1] - jnp.maximum(ham, 0.0)
                 pl.when(n < STEPS - 1)(lambda: pack(n + 1, c, r))
 
-            pl.when(n < STEPS - 1)(lambda: send_chunk(n + 1, c))
-            pl.when((n < STEPS - 1) & (i == 1))(lambda: send_y(n + 1))
-
-        pl.when(n < STEPS - 1)(lambda: send_x(n + 1))
+            @pl.when(n < STEPS - 1)
+            def _():
+                send_chunk(n + 1, c)
+                send_x(n + 1, c)
+                pl.when(i == 2)(lambda: send_y(n + 1, True))
+                pl.when(i == 3)(lambda: send_y(n + 1, False))
 
     @pl.loop(0, cy)
     def _(y):
@@ -436,13 +435,15 @@
 
     @pl.loop(0, STEPS)
     def _(n):
-        xu, xd = x_copies(n)
         yu, yd = y_copies(n)
         pl.when(has_yd)(lambda: yu.wait_send())
         pl.when(has_yu)(lambda: yd.wait_send())
-        pl.when(has_xd)(lambda: xu.wait_send())
-        pl.when(has_xu)(lambda: xd.wait_send())
-        for c in range(CHUNKS):
+
+        @pl.loop(0, CHUNKS)
+        def _(c):
+            xu, xd = x_copies(n, c)
+            pl.when(has_xd)(lambda: xu.wait_send())
+            pl.when(has_xu)(lambda: xd.wait_send())
             for copy in h_copies(n, c):
                 copy.wait_send()
 
@@ -499,7 +500,7 @@
                 pltpu.SMEM((total, 1, 128), i32),
                 pltpu.SMEM((total, 1, 128), f32),
                 pltpu.VMEM((total, CAP, 128), f32),
-                dma((nj,)), dma((nj,)), dma((STEPS, 4 + 2 * CHUNKS)), dma((STEPS, 4 + 2 * CHUNKS)),
+                dma((nj,)), dma((nj,)), dma((STEPS, 2 + 4 * CHUNKS)), dma((STEPS, 2 + 4 * CHUNKS)),
                 dma((total,)), dma((total,)), dma((total,)), dma((total,)),
                 dma((total,)), dma((total,)), dma((3,)),
             ],

time: 78.1 us -> 79.7 us (1.020)
  Pallas kernels: 70.5 us -> 72.1 us
    pallas_call x1, Pallas kernels: 70.5 us -> 72.1 us  [local(): pl.pallas_call(functools.partial(kernel, (ngx, ngy, nha, cx, cy, nj)), ou...]
where the time goes in v4:
time: 79.7 us; the launch traced here: 79.3 us
  Pallas kernels  72.1 us (90%)
  local copies, waits for them, and re-layouts  5.05 us (6%)
  other arithmetic  1.53 us (2%)
    pallas_call x1, Pallas kernels, local(): pl.pallas_call(functools.partial(kernel, (ngx, ngy, nha, cx, cy, nj)), ou...  72.1 us
    unnamed x5, local copies, waits for them, and re-layouts  2.91 us

profile of v4, /device:TPU:0, one launch (start us, length us, event | category | flops | bytes accessed | tf_op | source)
XLA Modules:
  0.0 79.3 jit_solution(2173926655918839900)
XLA Ops:
  0.6 0.0 copy-start
  0.6 0.8 copy.11
  1.4 0.6 pad.8
  2.0 0.0 copy-done
  2.0 0.1 copy.13
  2.1 0.6 pad.9
  2.7 72.1 %shard_map.59 = (f32[256,1024]{1,0:T(8,128)}, f32[32,4,128]{2,1,0:T(4,128)}) custom-call(f32[256,1024]{1,0:T(8,128)} %bitcast.13, s32[32,1,128]{2,1,0:T(1,128)} %bitcast.16, f32[32,1,128]{2,1,0:T(1,128)} %bitcast.17, f32[4,2,8,128]{3,2,1,0:T(8,128)} %constant.8.clone.drift_ref), custom_call_target="tpu_custom_call" | custom-call | tf_op jit(solution)/shard_map/pallas_call | solution.py:484
  74.8 0.9 %reduce_sum.9 = f32[32,4]{1,0:T(8,128)S(1)} reduce(f32[32,4,128]{2,1,0:T(4,128)} %get-tuple-element.5, f32[]{:T(128)} %constant.2.clone.1), dimensions={2}, to_apply=%region_0.1 | reduce | flops 16256 | bytes 66052 | tf_op jit(solution)/shard_map/reduce_sum | solution.py:510
  75.7 0.0 copy-start.1
  75.8 0.1 copy.14
  75.8 0.6 copy-done.1
  76.4 0.6 bitcast_select_fusion
  77.0 2.3 %copy.16 = f32[16,16,1024]{2,1,0:T(8,128)} copy(f32[16,16,1024]{2,1,0:T(8,128)} %bitcast.14) | data formatting | bytes 2097152
  (1 shorter events, 0.0 us)
Async XLA Ops:
  0.6 1.4 %copy-start = (f32[1,16,4,32]{3,2,1,0:T(4,128)S(1)}, f32[1,16,4,32]{3,2,1,0:T(4,128)}, u32[]{:S(2)}) copy-start(f32[1,16,4,32]{3,2,1,0:T(4,128)} %param.6) | copy-start | bytes 24580
  75.7 0.7 copy-start.1

commit v5 on v4

--- a/solution.py
+++ b/solution.py
@@ -69,8 +69,8 @@
     return forward, negated
 
 
-def kernel(sizes, v_hbm, code_ref, wt_ref, drift_ref, out_hbm, res_ref,
-           grid, hx, hy, moved, stage, send_h, recv_h, code_in, wt_in, code_s, wt_s, rows,
+def kernel(sizes, v_hbm, code_ref, wt_ref, drift_ref, corner_ref, out_hbm, res_ref,
+           grid, hx, hy, moved, stage, send_h, recv_h, code_in, wt_in, code_s, wt_s, rows, res_in, wt_tile,
            in_sem, out_sem, halo_send, halo_recv, cs_sem, cr_sem, ws_sem, wr_sem, rs_sem, rr_sem, loc_sem):
     ngx, ngy, nha, cx, cy, nj = sizes
     total = ngx * ngy * nha
@@ -329,6 +329,36 @@
             for k in range(cx):
                 hx[y, x0 + sx * k] = drift_x * line[k]
 
+    ramp = (lax.broadcasted_iota(jnp.int32, (8, 128), 0) * 128
+            + lax.broadcasted_iota(jnp.int32, (8, 128), 1))
+    hv = nj * 128
+
+    def get_requests():
+        @pl.loop(1, total)
+        def _(i):
+            for c in request_from((me + i) % total):
+                c.wait()
+
+        to_s = (pltpu.make_async_copy(code_in, code_s, loc_sem.at[0]),
+                pltpu.make_async_copy(wt_in, wt_s, loc_sem.at[1]))
+        for c in to_s:
+            c.start()
+        for c in to_s:
+            c.wait()
+
+    def weight_tiles(n):
+        @pl.loop(0, total // STEPS)
+        def _(q):
+            o = n * (total // STEPS) + q
+            for slot in range(CAP):
+                at = ramp - lax.rem(jnp.maximum(code_s[o, 0, slot], 0), hv)
+                hits = [at == off for off in (0, 1, NV, NV + 1)]
+                for m in range(4):
+                    w = jnp.zeros((8, 128), jnp.float32)
+                    for k in range(4):
+                        w = jnp.where(hits[k], wt_s[o, 0, slot * 16 + 4 * m + k], w)
+                    wt_tile[o * CAP + slot, m] = w
+
     @pl.loop(0, STEPS)
     def _(n):
         @pl.loop(0, CHUNKS)
@@ -362,6 +392,14 @@
                     grid[n + 1, y + LO, x + LO, 8:16, :] = g[1] - jnp.maximum(ham, 0.0)
                 pl.when(n < STEPS - 1)(lambda: pack(n + 1, c, r))
 
+            @pl.when(n == STEPS - 1)
+            def _():
+                @pl.loop(0, depth)
+                def _(r):
+                    y = c * depth + r
+                    for x in range(cx):
+                        stage[pl.ds(x * cy + y, nj, stride=cx * cy), :] = grid[STEPS, y + LO, x + LO, 8:16, :]
+
             @pl.when(n < STEPS - 1)
             def _():
                 send_chunk(n + 1, c)
@@ -369,11 +407,8 @@
                 pl.when(i == 2)(lambda: send_y(n + 1, True))
                 pl.when(i == 3)(lambda: send_y(n + 1, False))
 
-    @pl.loop(0, cy)
-    def _(y):
-        for x in range(cx):
-            row = x * cy + y
-            stage[pl.ds(row, nj, stride=cx * cy), :] = grid[STEPS, y + LO, x + LO, 8:16, :]
+            pl.when((n == 0) & (i == 2))(get_requests)
+            pl.when(i == 2)(lambda: weight_tiles(n))
 
     stores = [
         pltpu.make_async_copy(
@@ -383,25 +418,9 @@
     for c in stores:
         c.start()
 
-    @pl.loop(1, total)
-    def _(i):
-        for c in request_from((me + i) % total):
-            c.wait()
-
-    to_s = (pltpu.make_async_copy(code_in, code_s, loc_sem.at[0]),
-            pltpu.make_async_copy(wt_in, wt_s, loc_sem.at[1]))
-    for c in to_s:
-        c.start()
-    for c in to_s:
-        c.wait()
-
-    ramp = (lax.broadcasted_iota(jnp.int32, (8, 128), 0) * 128
-            + lax.broadcasted_iota(jnp.int32, (8, 128), 1))
-    hv = nj * 128
-
     def answer(o, slot_of):
         return pltpu.make_async_remote_copy(
-            src_ref=rows.at[o], dst_ref=res_ref.at[slot_of], send_sem=rs_sem.at[o],
+            src_ref=rows.at[o], dst_ref=res_in.at[slot_of], send_sem=rs_sem.at[o],
             recv_sem=rr_sem.at[slot_of], device_id=device_of(o), device_id_type=MESH)
 
     @pl.loop(0, total)
@@ -409,22 +428,15 @@
         o = (me + i + 1) % total
         for slot in range(CAP):
             c = jnp.maximum(code_s[o, 0, slot], 0)
-            a = c // (cy * hv)
-            b = (c // hv) % cy
-            at = ramp - c % hv
-            hits = [at == off for off in (0, 1, NV, NV + 1)]
-            acc = None
-            for i1 in range(2):
-                for i2 in range(2):
-                    w = jnp.zeros((8, 128), jnp.float32)
-                    for k in range(4):
-                        w = jnp.where(hits[k], wt_s[o, 0, slot * 16 + 8 * i1 + 4 * i2 + k], w)
-                    part = w * grid[STEPS, b + i2 + LO, a + i1 + LO, 8:16, :]
-                    acc = part if acc is None else acc + part
+            a = lax.div(c, cy * hv)
+            b = lax.rem(lax.div(c, hv), cy)
+            part = [wt_tile[o * CAP + slot, 2 * i1 + i2] * grid[STEPS, b + i2 + LO, a + i1 + LO, 8:16, :]
+                    for i1 in range(2) for i2 in range(2)]
+            acc = (part[0] + part[1]) + (part[2] + part[3])
             rows[o, slot:slot + 1, :] = jnp.sum(acc, axis=0, keepdims=True)
         pl.when(o != me)(lambda: answer(o, me).start())
 
-    mine = pltpu.make_async_copy(rows.at[me], res_ref.at[me], loc_sem.at[2])
+    mine = pltpu.make_async_copy(rows.at[me], res_in.at[me], loc_sem.at[2])
     mine.start()
     mine.wait()
 
@@ -432,6 +444,10 @@
     def _(i):
         o = (me + i) % total
         answer(o, o).wait()
+
+    for slot in range(CAP):
+        sums = jnp.sum(res_in[:, slot, :].T, axis=0, keepdims=True)
+        res_ref[slot:slot + 1, :] = jnp.where(corner_ref[slot:slot + 1, :] >= 0, sums, 0.0)
 
     @pl.loop(0, STEPS)
     def _(n):
@@ -466,7 +482,7 @@
 def solution(mesh):
     ngx, ngy, nha = (mesh.shape[k] for k in ("gx", "gy", "ha"))
     total = ngx * ngy * nha
-    assert nha % 4 == 0
+    assert nha % 4 == 0 and total % STEPS == 0
 
     def local(initial_value, corner, weights):
         cx, cy, chv = initial_value.shape
@@ -481,11 +497,11 @@
         dma = pltpu.SemaphoreType.DMA
         vmem = pl.BlockSpec(memory_space=pltpu.VMEM)
         any_ = pl.BlockSpec(memory_space=pl.ANY)
-        final, parts = pl.pallas_call(
+        final, samples = pl.pallas_call(
             functools.partial(kernel, (ngx, ngy, nha, cx, cy, nj)),
             out_shape=(jax.ShapeDtypeStruct((cx * cy, chv), f32),
-                       jax.ShapeDtypeStruct((total, CAP, 128), f32)),
-            in_specs=[any_, vmem, vmem, vmem],
+                       jax.ShapeDtypeStruct((CAP, total), f32)),
+            in_specs=[any_, vmem, vmem, vmem, vmem],
             out_specs=(any_, vmem),
             scratch_shapes=[
                 pltpu.VMEM((STEPS + 1, cy + 2 * LO, cx + 2 * LO, 24, 128), f32),
@@ -500,15 +516,16 @@
                 pltpu.SMEM((total, 1, 128), i32),
                 pltpu.SMEM((total, 1, 128), f32),
                 pltpu.VMEM((total, CAP, 128), f32),
+                pltpu.VMEM((total, CAP, 128), f32),
+                pltpu.VMEM((total * CAP, 4, 8, 128), f32),
                 dma((nj,)), dma((nj,)), dma((STEPS, 2 + 4 * CHUNKS)), dma((STEPS, 2 + 4 * CHUNKS)),
                 dma((total,)), dma((total,)), dma((total,)), dma((total,)),
                 dma((total,)), dma((total,)), dma((3,)),
             ],
             compiler_params=pltpu.CompilerParams(
                 collective_id=0, has_side_effects=True, vmem_limit_bytes=56 * 1024 * 1024),
-        )(initial_value.reshape(cx * cy, chv), codes, wts, table)
-        sampled = jnp.sum(parts, axis=2).T[None]
-        return (final.reshape(cx, cy, chv), jnp.where(corner >= 0, sampled, 0.0))
+        )(initial_value.reshape(cx * cy, chv), codes, wts, table, corner[0])
+        return (final.reshape(cx, cy, chv), samples[None])
 
     return jax.shard_map(
         local,

time: 79.7 us -> 78.4 us (0.984)
  other arithmetic: 1.53 us -> 0 us
    reduce_sum x1 -> x0, other arithmetic: 0.95 us -> none  [local(): sampled = jnp.sum(parts, axis=2).T[None]]
    unnamed x5 -> x6, local copies, waits for them, and re-layouts: 2.91 us -> 2.89 us
where the time goes in v5:
time: 78.4 us; the launch traced here: 78.2 us
  Pallas kernels  72.5 us (92%)
  local copies, waits for them, and re-layouts  4.96 us (6%)
    pallas_call x1, Pallas kernels, local(): pl.pallas_call(functools.partial(kernel, (ngx, ngy, nha, cx, cy, nj)), ou...  72.5 us
    unnamed x6, local copies, waits for them, and re-layouts  2.89 us

profile of v5, /device:TPU:0, one launch (start us, length us, event | category | flops | bytes accessed | tf_op | source)
XLA Modules:
  0.0 78.2 jit_solution(10408751689015073873)
XLA Ops:
  0.6 0.0 copy-start
  0.6 0.8 copy.8
  1.4 0.6 pad.8
  2.0 0.0 copy-done
  2.0 0.1 copy.10
  2.1 0.6 pad.9
  2.7 72.5 %shard_map.59 = (f32[256,1024]{1,0:T(8,128)}, f32[4,32]{1,0:T(4,128)}) custom-call(f32[256,1024]{1,0:T(8,128)} %bitcast.11, s32[32,1,128]{2,1,0:T(1,128)} %bitcast.14, f32[32,1,128]{2,1,0:T(1,128)} %bitcast.15, f32[4,2,8,128]{3,2,1,0:T(8,128)} %constant.6.clone.drift_ref, s32[4,32]{1,0:T(4,128)} %bitcast.19), custom_call_target="tpu_custom_call" | custom-call | tf_op jit(solution)/shard_map/pallas_call | solution.py:500
  75.3 0.0 copy-start.1
  75.3 2.3 %copy.13 = f32[16,16,1024]{2,1,0:T(8,128)} copy(f32[16,16,1024]{2,1,0:T(8,128)} %bitcast.12) | data formatting | bytes 2097152
  77.6 0.0 copy-done.1
  77.6 0.6 copy.14
  (1 shorter events, 0.0 us)
Async XLA Ops:
  0.6 1.4 %copy-start = (f32[1,16,4,32]{3,2,1,0:T(4,128)S(1)}, f32[1,16,4,32]{3,2,1,0:T(4,128)}, u32[]{:S(2)}) copy-start(f32[1,16,4,32]{3,2,1,0:T(4,128)} %param.6) | copy-start | bytes 24580
  75.3 2.3 %copy-start.1 = (f32[4,32]{1,0:T(4,128)S(1)}, f32[4,32]{1,0:T(4,128)}, u32[]{:S(2)}) copy-start(f32[4,32]{1,0:T(4,128)} %get-tuple-element.5) | copy-start | bytes 1540

commit v6 on v5

--- a/solution.py
+++ b/solution.py
@@ -22,8 +22,7 @@
     return (13.0 / 3.0) * (t * t) + EPS4
 
 
-def weight(v):
-    v = pl.reciprocal(v, approx=True)
+def square(v):
     return v * v
 
 
@@ -38,18 +37,19 @@
     return d, e, z, m, e3
 
 
-def weights_at(i, e, m, e3):
+def products_at(i, e, m, e3):
     u1 = e3[i + 1] - e[i]
     u2 = e[i + 1] + e[i + 2]
     u3 = e3[i + 2] - e[i + 3]
-    return weight(m[i] + u1 * u1), 6.0 * weight(m[i + 1] + u2 * u2), weight(m[i + 2] + u3 * u3)
+    s1, s2, s3 = square(m[i] + u1 * u1), square(m[i + 1] + u2 * u2), square(m[i + 2] + u3 * u3)
+    return s2 * s3, 6.0 * (s1 * s3), s1 * s2
 
 
 def upwind_line(cells):
     d, e, z, m, e3 = terms(cells)
     out = []
     for i in range(len(cells) - 5):
-        g1, g2, g3 = weights_at(i, e, m, e3)
+        g1, g2, g3 = products_at(i, e, m, e3)
         g3 = 3.0 * g3
         num = (z[i] + z[i]) * g1 + z[i + 1] * g3
         lin = 6.0 * d[i + 2] + (e[i + 1] + (e[i + 2] + e[i + 2]))
@@ -59,7 +59,7 @@
 
 def both_ways(cells):
     d, e, z, m, e3 = terms(cells)
-    g1, g2, g3 = weights_at(0, e, m, e3)
+    g1, g2, g3 = products_at(0, e, m, e3)
     c = 6.0 * d[2]
     h1, h3 = 3.0 * g1, 3.0 * g3
     forward = (c + (e[1] + (e[2] + e[2]))
@@ -315,11 +315,13 @@
     drift_y = drift_ref[ha, 1]
 
     def y_part(n, first, count):
-        @pl.loop(0, cx)
-        def _(x):
-            line = upwind_line([grid[n, yb + sy * (first + i), x + LO, 8:16, :] for i in range(count + 5)])
-            for k in range(count):
-                hy[y0 + sy * (first + k), x] = drift_y * line[k]
+        @pl.loop(0, cx // 4)
+        def _(q):
+            for p in range(4):
+                x = 4 * q + p
+                line = upwind_line([grid[n, yb + sy * (first + i), x + LO, 8:16, :] for i in range(count + 5)])
+                for k in range(count):
+                    hy[y0 + sy * (first + k), x] = drift_y * line[k]
 
     def x_part(n, c):
         @pl.loop(0, depth)

time: 78.4 us -> 74.5 us (0.950)
  Pallas kernels: 72.5 us -> 68.6 us
    pallas_call x1, Pallas kernels: 72.5 us -> 68.6 us  [local(): pl.pallas_call(functools.partial(kernel, (ngx, ngy, nha, cx, cy, nj)), ou...]
where the time goes in v6:
time: 74.5 us; the launch traced here: 74.2 us
  Pallas kernels  68.6 us (92%)
  local copies, waits for them, and re-layouts  4.96 us (7%)
    pallas_call x1, Pallas kernels, local(): pl.pallas_call(functools.partial(kernel, (ngx, ngy, nha, cx, cy, nj)), ou...  68.6 us
    unnamed x6, local copies, waits for them, and re-layouts  2.89 us

profile of v6, /device:TPU:0, one launch (start us, length us, event | category | flops | bytes accessed | tf_op | source)
XLA Modules:
  0.0 74.2 jit_solution(7430631691650356495)
XLA Ops:
  0.6 0.0 copy-start
  0.6 0.8 %copy.8 = s32[4,32]{0,1:T(8,128)S(1)} copy(s32[4,32]{1,0:T(4,128)} %bitcast.18) | data formatting | bytes 1024 | tf_op jit(solution)/shard_map/squeeze | solution.py:494
  1.4 0.6 pad.8
  2.0 0.0 copy-done
  2.0 0.1 copy.10
  2.1 0.6 pad.9
  2.7 68.6 %shard_map.59 = (f32[256,1024]{1,0:T(8,128)}, f32[4,32]{1,0:T(4,128)}) custom-call(f32[256,1024]{1,0:T(8,128)} %bitcast.11, s32[32,1,128]{2,1,0:T(1,128)} %bitcast.14, f32[32,1,128]{2,1,0:T(1,128)} %bitcast.15, f32[4,2,8,128]{3,2,1,0:T(8,128)} %constant.6.clone.drift_ref, s32[4,32]{1,0:T(4,128)} %bitcast.19), custom_call_target="tpu_custom_call" | custom-call | tf_op jit(solution)/shard_map/pallas_call | solution.py:502
  71.3 0.0 copy-start.1
  71.3 2.3 %copy.13 = f32[16,16,1024]{2,1,0:T(8,128)} copy(f32[16,16,1024]{2,1,0:T(8,128)} %bitcast.12) | data formatting | bytes 2097152
  73.6 0.0 copy-done.1
  73.7 0.6 copy.14
  (1 shorter events, 0.0 us)
Async XLA Ops:
  0.6 1.4 %copy-start = (f32[1,16,4,32]{3,2,1,0:T(4,128)S(1)}, f32[1,16,4,32]{3,2,1,0:T(4,128)}, u32[]{:S(2)}) copy-start(f32[1,16,4,32]{3,2,1,0:T(4,128)} %param.6) | copy-start | bytes 24580
  71.3 2.3 %copy-start.1 = (f32[4,32]{1,0:T(4,128)S(1)}, f32[4,32]{1,0:T(4,128)}, u32[]{:S(2)}) copy-start(f32[4,32]{1,0:T(4,128)} %get-tuple-element.5) | copy-start | bytes 1540

commit v7 on v6

--- a/solution.py
+++ b/solution.py
@@ -70,7 +70,7 @@
 
 
 def kernel(sizes, v_hbm, code_ref, wt_ref, drift_ref, corner_ref, out_hbm, res_ref,
-           grid, hx, hy, moved, stage, send_h, recv_h, code_in, wt_in, code_s, wt_s, rows, res_in, wt_tile,
+           grid, hx, hy, moved, turned, stage, send_h, recv_h, code_in, wt_in, code_s, wt_s, rows, res_in, wt_tile,
            in_sem, out_sem, halo_send, halo_recv, cs_sem, cr_sem, ws_sem, wr_sem, rs_sem, rr_sem, loc_sem):
     ngx, ngy, nha, cx, cy, nj = sizes
     total = ngx * ngy * nha
@@ -225,6 +225,7 @@
     flat = grid.reshape(grid.shape[0] * grid.shape[1] * grid.shape[2] * 24, 128)
 
     moved_flat = moved.reshape(cx * 24, 128)
+    turned_flat = turned.reshape(cx * 24, 128)
 
     def row_of(n, y, x, r):
         return ((n * (cy + 2 * LO) + y + LO) * (cx + 2 * LO) + x + LO) * 24 + r
@@ -250,6 +251,8 @@
         for q in range(2 * halves):
             flat[pl.ds(row_of(n, y, 8 * q, 7), 8, stride=24), :] = recv_h[n, 0, c, r * 2 * halves + q]
             flat[pl.ds(row_of(n, y, 8 * q, 16), 8, stride=24), :] = recv_h[n, 1, c, r * 2 * halves + q]
+            turned_flat[pl.ds(8 * q * 24 + 7, 8, stride=24), :] = swap(recv_h[n, 0, c, r * 2 * halves + q])
+            turned_flat[pl.ds(8 * q * 24 + 16, 8, stride=24), :] = swap(recv_h[n, 1, c, r * 2 * halves + q])
         for q in range(halves):
             at = (2 * depth + r) * halves + q
             v = recv_h[n, 0, c, at]
@@ -264,8 +267,8 @@
             moved_flat[pl.ds(16 * q * 24 + 7, 8, stride=24), :] = edge
             moved_flat[pl.ds((16 * q + 8) * 24 + 7, 8, stride=24), :] = swap(edge)
             v = recv_h[n, 1, c, at]
-            flat[pl.ds(row_of(n, y, 16 * q, 17), 8, stride=24), :] = v
-            flat[pl.ds(row_of(n, y, 16 * q + 8, 17), 8, stride=24), :] = swap(v)
+            turned_flat[pl.ds(16 * q * 24 + 17, 8, stride=24), :] = swap(v)
+            turned_flat[pl.ds((16 * q + 8) * 24 + 17, 8, stride=24), :] = v
 
     def send_chunk(n, c):
         for copy in h_copies(n, c):
@@ -382,8 +385,10 @@
                 y = c * depth + r
                 unpack(n, c, r)
                 for x in range(cx):
-                    g = [grid[n, y + LO, x + LO, pl.ds(k, 8), :] for k in range(7, 11)]
-                    s = [swap(v) for v in g]
+                    g = [grid[n, y + LO, x + LO, pl.ds(k, 8), :] for k in range(7, 10)]
+                    mid = swap(g[1])
+                    turned[x, 8:16, :] = mid
+                    s = [turned[x, 7:15, :], mid, turned[x, 9:17, :], turned[x, 10:18, :]]
                     odd = [jnp.where(low_half, s[k], s[k + 1]) for k in range(3)]
                     forward, negated = both_ways([g[0], odd[0], g[1], odd[1], g[2], odd[2]])
                     forward = swap(forward)
@@ -510,6 +515,7 @@
                 pltpu.VMEM((cy, cx, 8, 128), f32),
                 pltpu.VMEM((cy, cx, 8, 128), f32),
                 pltpu.VMEM((cx, 24, 128), f32),
+                pltpu.VMEM((cx, 24, 128), f32),
                 pltpu.VMEM((nj * cx * cy, 128), f32),
                 pltpu.VMEM((STEPS, 2, CHUNKS, tiles // CHUNKS, 8, 128), f32),
                 pltpu.VMEM((STEPS, 2, CHUNKS, tiles // CHUNKS, 8, 128), f32),

time: 74.5 us -> 71.6 us (0.961)
  Pallas kernels: 68.6 us -> 65.7 us
    pallas_call x1, Pallas kernels: 68.6 us -> 65.7 us  [local(): pl.pallas_call(functools.partial(kernel, (ngx, ngy, nha, cx, cy, nj)), ou...]
where the time goes in v7:
time: 71.6 us; the launch traced here: 71.3 us
  Pallas kernels  65.7 us (92%)
  local copies, waits for them, and re-layouts  4.96 us (7%)
    pallas_call x1, Pallas kernels, local(): pl.pallas_call(functools.partial(kernel, (ngx, ngy, nha, cx, cy, nj)), ou...  65.7 us
    unnamed x6, local copies, waits for them, and re-layouts  2.89 us

profile of v7, /device:TPU:0, one launch (start us, length us, event | category | flops | bytes accessed | tf_op | source)
XLA Modules:
  0.0 71.3 jit_solution(17113406439287241830)
XLA Ops:
  0.6 0.0 copy-start
  0.6 0.8 %copy.8 = s32[4,32]{0,1:T(8,128)S(1)} copy(s32[4,32]{1,0:T(4,128)} %bitcast.18) | data formatting | bytes 1024 | tf_op jit(solution)/shard_map/squeeze | solution.py:499
  1.4 0.6 pad.8
  2.0 0.0 copy-done
  2.0 0.1 copy.10
  2.1 0.6 pad.9
  2.7 65.7 %shard_map.59 = (f32[256,1024]{1,0:T(8,128)}, f32[4,32]{1,0:T(4,128)}) custom-call(f32[256,1024]{1,0:T(8,128)} %bitcast.11, s32[32,1,128]{2,1,0:T(1,128)} %bitcast.14, f32[32,1,128]{2,1,0:T(1,128)} %bitcast.15, f32[4,2,8,128]{3,2,1,0:T(8,128)} %constant.6.clone.drift_ref, s32[4,32]{1,0:T(4,128)} %bitcast.19), custom_call_target="tpu_custom_call" | custom-call | tf_op jit(solution)/shard_map/pallas_call | solution.py:507
  68.4 0.0 copy-start.1
  68.4 2.3 %copy.13 = f32[16,16,1024]{2,1,0:T(8,128)} copy(f32[16,16,1024]{2,1,0:T(8,128)} %bitcast.12) | data formatting | bytes 2097152
  70.7 0.0 copy-done.1
  70.7 0.6 copy.14
  (1 shorter events, 0.0 us)
Async XLA Ops:
  0.6 1.4 %copy-start = (f32[1,16,4,32]{3,2,1,0:T(4,128)S(1)}, f32[1,16,4,32]{3,2,1,0:T(4,128)}, u32[]{:S(2)}) copy-start(f32[1,16,4,32]{3,2,1,0:T(4,128)} %param.6) | copy-start | bytes 24580
  68.4 2.3 %copy-start.1 = (f32[4,32]{1,0:T(4,128)S(1)}, f32[4,32]{1,0:T(4,128)}, u32[]{:S(2)}) copy-start(f32[4,32]{1,0:T(4,128)} %get-tuple-element.5) | copy-start | bytes 1540
